TPU v7x, 512 devices: a whole 4x8x8 slice. The times are simulated.
512 devices in a mesh: rep: 16 (over y, x_lo), fsdp: 8 (over z), tp: 4 (over x_hi, core).
Axes of the slice: x: 4 (x_hi: 2, x_lo: 2; x = x_hi * 2 + x_lo), y: 8, z: 8, core: 2. Of those that a mesh axis runs over, the one named last changes fastest.
Arguments:
- grad_parts: bfloat16 [8, 2, 8192, 1024], P('fsdp', None, 'rep', 'tp'), may hold values from -4 to 4
- master_weight: float32 [2, 8192, 1024], P(None, ('rep', 'fsdp'), 'tp'), may hold values from -0.0625 to 0.0625
- moment_one: float32 [2, 8192, 1024], P(None, ('rep', 'fsdp'), 'tp'), may hold values from -4 to 4
- moment_two: float32 [2, 8192, 1024], P(None, ('rep', 'fsdp'), 'tp'), may hold values from 0.1 to 2
- layer_inputs: bfloat16 [6144, 4, 8192], P(('rep', 'fsdp'), None, 'tp'), may hold values from -6 to 6
- queries: bfloat16 [6144, 4, 8192], P(('rep', 'fsdp'), None, 'tp'), may hold values from -105 to 105
- kv_cache: bfloat16 [6144, 24, 2, 1024], P(('rep', 'fsdp'), None, None, 'tp'), may hold values from -4 to 4
- lengths: int32 [6144], P(('rep', 'fsdp')), may hold values from 2 to 24
Outputs:
- new_master: float32 [2, 8192, 1024], P(None, ('rep', 'fsdp'), 'tp')
- new_moment_one: float32 [2, 8192, 1024], P(None, ('rep', 'fsdp'), 'tp')
- new_moment_two: float32 [2, 8192, 1024], P(None, ('rep', 'fsdp'), 'tp')
- context: bfloat16 [6144, 4, 8192], P(('rep', 'fsdp'), None, 'tp')
Inputs may be any that keep to these rules, and one draw needn't show every extreme that they name: lengths[r] is the number of valid cached positions of row r, at most 24.
All inputs are finite; a program needn't handle non-finite values.
Results may differ from a plain program's by a relative error of at most 0.0065.
Values may be sent and summed in bfloat16 or wider, within the bound.
No kernel may reach another device: no remote copies, remote signals or barrier semaphores. Data moves between devices by JAX's collectives and lax.ppermute only.
A program may use at most 64 MiB of HBM per device.

v0:
```python
import jax
import jax.numpy as jnp
from jax import lax
from jax.sharding import Mesh
from jax.sharding import PartitionSpec as P

HD = 128
REP_FSDP = ("rep_0", "rep_1", "fsdp")
REP = ("rep_0", "rep_1")


beta_one = 0.9
beta_two = 0.95
learning_rate = 0.001
weight_decay = 0.1
epsilon = 1e-08
first_bias = 1.0 - 0.9**10
second_bias = 1.0 - 0.95**10


def split_up(x, dim, size):
    dims = x.shape
    parts = x.reshape(*dims[:dim], size, dims[dim] // size, *dims[dim + 1 :])
    return jnp.moveaxis(parts, dim, 0)


def sent_and_summed(x, axis, dim):
    size = lax.axis_size(axis)
    parts = lax.all_to_all(split_up(x, dim, size), axis, 0, 0, tiled=True)
    return jnp.sum(parts.astype(jnp.float32), axis=0)


def in_order(parts, dim):
    dims = list(parts.shape[1:])
    dims[dim] *= parts.shape[0]
    return jnp.moveaxis(parts, 0, dim).reshape(dims)


def all_blocks(x, axes, turns):
    parts = x
    for k in turns:
        parts = lax.all_gather(parts, axes[k])
    done = turns[::-1]
    back = [done.index(k) for k in range(len(axes))]
    parts = parts.transpose(*back, *range(len(axes), parts.ndim))
    return parts.reshape(-1, *x.shape)


def whole_of(x, axes, turns, dim):
    return in_order(all_blocks(x, axes, turns), dim)


def adamw_update(gradient, master, moment_one, moment_two):
    new_one = beta_one * moment_one + (1.0 - beta_one) * gradient
    new_two = beta_two * moment_two + (1.0 - beta_two) * gradient * gradient
    update = new_one / first_bias / (jnp.sqrt(new_two / second_bias) + epsilon)
    new_master = master - learning_rate * (update + weight_decay * master)
    return (new_one, new_two, new_master)


def attend(queries, kv_cache, fresh_keys, fresh_values, lengths):
    row_count = queries.shape[0]
    step_count = queries.shape[1]
    kv_heads = fresh_keys.shape[2]
    cache_len = kv_cache.shape[1]
    grouped = queries.reshape(row_count, step_count, kv_heads, -1, HD)
    cached_keys = kv_cache[:, :, 0].reshape(row_count, cache_len, kv_heads, HD)
    cached_values = kv_cache[:, :, 1].reshape(row_count, cache_len, kv_heads, HD)
    scaling = 1.0 / jnp.sqrt(jnp.float32(HD))
    cached_scores = (
        jnp.einsum("rsgqd,rcgd->rsgqc", grouped, cached_keys, preferred_element_type=jnp.float32)
        * scaling
    )
    fresh_scores = (
        jnp.einsum("rsgqd,rugd->rsgqu", grouped, fresh_keys, preferred_element_type=jnp.float32)
        * scaling
    )
    valid_old = jnp.arange(cache_len, dtype=jnp.int32)[None, :] < lengths[:, None]
    valid_old = valid_old[:, None, None, None, :]
    steps_index = jnp.arange(step_count, dtype=jnp.int32)
    valid_new = (steps_index[None, :] <= steps_index[:, None])[None, :, None, None, :]
    scores = jnp.concatenate(
        [
            jnp.where(valid_old, cached_scores, -jnp.inf),
            jnp.where(valid_new, fresh_scores, -jnp.inf),
        ],
        axis=-1,
    )
    row_max = jnp.max(scores, axis=-1, keepdims=True)
    exponent = jnp.exp(scores - row_max)
    weights = (exponent / jnp.sum(exponent, axis=-1, keepdims=True)).astype(jnp.bfloat16)
    output = jnp.einsum(
        "rsgqc,rcgd->rsgqd",
        weights[..., :cache_len],
        cached_values,
        preferred_element_type=jnp.float32,
    )
    output = output + jnp.einsum(
        "rsgqu,rugd->rsgqd",
        weights[..., cache_len:],
        fresh_values,
        preferred_element_type=jnp.float32,
    )
    return output.astype(jnp.bfloat16).reshape(row_count, step_count, -1)


def on_device(
    grad_parts, master_weight, moment_one, moment_two, layer_inputs, queries, kv_cache, lengths
):
    gradient = sent_and_summed(grad_parts[0].astype(jnp.float32).astype(jnp.bfloat16), "fsdp", 1)
    new_one, new_two, new_master = adamw_update(gradient, master_weight, moment_one, moment_two)
    rollout_weight = new_master.astype(jnp.bfloat16)
    row_count = layer_inputs.shape[0]
    step_count = layer_inputs.shape[1]
    gathered = lax.all_gather(layer_inputs, "tp", axis=2, tiled=True)
    flattened = gathered.reshape(row_count * step_count, gathered.shape[2])
    projected = jnp.einsum(
        "td,kdc->ktc",
        flattened,
        whole_of(rollout_weight, REP_FSDP, (1, 0, 2), 1),
        preferred_element_type=jnp.float32,
    )
    fresh_pair = projected.astype(jnp.bfloat16).reshape(2, row_count, step_count, -1, HD)
    context = attend(queries, kv_cache, fresh_pair[0], fresh_pair[1], lengths)
    return (new_master, new_one, new_two, context)


def solution(mesh):
    finer = Mesh(
        mesh.devices.reshape(8, 2, mesh.shape["fsdp"], mesh.shape["tp"]),
        ("rep_0", "rep_1", "fsdp", "tp"),
    )
    return jax.shard_map(
        on_device,
        mesh=finer,
        in_specs=(
            P("fsdp", None, REP, "tp"),
            P(None, REP_FSDP, "tp"),
            P(None, REP_FSDP, "tp"),
            P(None, REP_FSDP, "tp"),
            P(REP_FSDP, None, "tp"),
            P(REP_FSDP, None, "tp"),
            P(REP_FSDP, None, None, "tp"),
            P(REP_FSDP),
        ),
        out_specs=(
            P(None, REP_FSDP, "tp"),
            P(None, REP_FSDP, "tp"),
            P(None, REP_FSDP, "tp"),
            P(REP_FSDP, None, "tp"),
        ),
        check_vma=False,
    )
```

profile of v0, /device:TPU:1, one launch (start us, length us, event | category | flops | bytes accessed | tf_op | source)
XLA Modules:
  0.0 261.9 jit_solution(16892887311878744765)
XLA Ops:
  7.2 0.0 copy-start.6
  7.2 0.0 copy-start.7
  7.2 0.0 copy-start.5
  7.2 0.0 all-gather.9.cloned.1.call-start
  7.2 1.2 copy.94
  8.4 26.7 %all_to_all.5 = bf16[8,2,64,256]{3,2,1,0:T(8,128)(2,1)S(1)} all-to-all(bf16[8,2,64,256]{3,2,1,0:T(8,128)(2,1)S(1)} %copy.94), channel_id=1, replica_groups=mesh['rep_0'=8,'rep_1'=2,'fsdp'=8,'tp'=4] {'fsdp'}, dimensions={0} | all-to-all | bytes 1048576 | tf_op jit(solution)/shard_map/all_to_all | solution.py:29
  35.1 0.1 convert_reduce_fusion
  35.2 0.0 copy-done.6
  35.2 0.0 copy-done.7
  35.2 0.0 copy-done.5
  35.2 0.0 copy-start.3
  35.2 0.8 fusion.16
  36.0 3.9 %all-gather = bf16[4,64,256]{2,1,0:T(8,128)(2,1)} all-gather(bf16[2,64,256]{2,1,0:T(8,128)(2,1)S(1)} %get-tuple-element.36), channel_id=2, replica_groups=mesh['rep_0'=8,'rep_1'=2,'fsdp'=8,'tp'=4] {'rep_1'}, dimensions={0}, use_global_device_ids=true | all-gather | bytes 196608 | tf_op jit(solution)/shard_map/all_gather | solution.py:42
  39.9 0.0 all-gather.9.cloned.1.call-update
  39.9 0.0 copy-start.1
  39.9 0.0 all-gather.7.cloned.1.call-start
  40.0 0.7 all-gather.7.cloned.1.call-update
  40.7 0.0 all-gather.11.cloned.1.call-start
  40.7 35.4 %all-gather.9.cloned.1.call-done = bf16[16,2,64,256]{3,2,1,0:T(8,128)(2,1)} async-done(((bf16[2,2,64,256]{3,2,1,0:T(8,128)(2,1)}), bf16[16,2,64,256]{3,2,1,0:T(8,128)(2,1)}) %all-gather.9.cloned.1.call-update) | async-done | bytes 1048592 | tf_op jit(solution)/shard_map/all_gather | solution.py:42
  76.1 0.0 all-gather.11.cloned.1.call-update
  76.2 0.0 copy-done.3
  76.2 0.5 reshape.68
  76.7 0.0 copy-done.1
  76.7 4.9 %slice_reduce_fusion = (bf16[48,24,256]{2,1,0:T(8,128)(2,1)S(1)}, bf16[48,24,256]{2,1,0:T(8,128)(2,1)S(1)}) fusion(bf16[48,24,2,256]{3,2,1,0:T(2,128)(2,1)S(1)} %copy-done.1), kind=kLoop, calls=%fused_computation.6 | loop fusion | bytes 2359296 | tf_op jit(solution)/shard_map/slice | solution.py:68
  81.6 0.0 copy-start.8
  81.6 1.0 reshape_squeeze.6
  82.6 0.9 reshape_squeeze.7
  83.5 0.0 copy-done.8
  83.5 0.1 iota_compare_fusion
  83.6 1.7 fusion.19
  85.3 34.1 %all-gather.7.cloned.1.call-done = bf16[48,4,8192]{2,1,0:T(4,128)(2,1)} async-done(((bf16[48,4,2048]{2,1,0:T(4,128)(2,1)}), bf16[48,4,8192]{2,1,0:T(4,128)(2,1)}) %all-gather.7.cloned.1.call-update) | async-done | bytes 3145744 | tf_op jit(solution)/shard_map/all_gather | solution.py:115
  119.4 5.5 %reshape.77 = bf16[192,8192,1]{1,0,2:T(8,128)(2,1)} reshape(bf16[48,4,8192]{2,1,0:T(4,128)(2,1)} %all-gather.7.cloned.1.call-done) | data formatting | bytes 6291456 | tf_op jit(solution)/shard_map/reshape | solution.py:116
  124.9 93.3 %all-gather.11.cloned.1.call-done = bf16[64,2,2,64,256]{4,3,2,1,0:T(8,128)(2,1)} async-done(((bf16[8,2,2,64,256]{4,3,2,1,0:T(8,128)(2,1)}), bf16[64,2,2,64,256]{4,3,2,1,0:T(8,128)(2,1)}) %all-gather.11.cloned.1.call-update) | async-done | bytes 8388624 | tf_op jit(solution)/shard_map/all_gather | solution.py:42
  218.2 8.3 %copy.97 = bf16[8,2,8,2,64,256]{5,4,3,2,1,0:T(8,128)(2,1)} copy(bf16[8,2,8,2,64,256]{5,4,3,1,0,2:T(8,128)(2,1)} %bitcast.34) | data formatting | bytes 16777216 | tf_op jit(solution)/shard_map/transpose | solution.py:45
  226.5 0.0 copy-start.2
  226.5 8.4 %copy.98 = bf16[2,128,64,256]{3,2,1,0:T(8,128)(2,1)} copy(bf16[2,128,64,256]{3,2,0,1:T(8,128)(2,1)} %bitcast.33) | data formatting | bytes 16777216 | tf_op jit(solution)/shard_map/transpose | solution.py:36
  234.9 0.0 copy-done.2
  234.9 5.3 %fusion.2 = bf16[2,192,256]{2,1,0:T(8,128)(2,1)S(1)} fusion(bf16[192,8192,1]{1,0,2:T(8,128)(2,1)S(1)} %copy-done.2, bf16[2,8192,256]{2,1,0:T(8,128)(2,1)} %bitcast.35), kind=kOutput, calls=%fused_computation.9 | convolution fusion | flops 1610711040 | bytes 11730944 | tf_op jit(solution)/shard_map/td,kdc->ktc/dot_general | solution.py:117
  240.2 0.6 fusion.18
  240.9 3.5 %fusion.6 = f32[48,2,4,4,8]{4,2,3,1,0:T(4,128)S(1)} fusion(bf16[48,4,2,8,128]{4,3,2,1,0:T(8,128)(2,1)S(1)} %reshape.68, bf16[48,4,2,128,1]{3,2,1,0,4:T(2,128)(2,1)S(1)} %bitcast.42), kind=kOutput, calls=%fused_computation.14 | convolution fusion | flops 3145728 | bytes 933888 | tf_op jit(solution)/shard_map/rsgqd,rugd->rsgqu/dot_general | solution.py:75
  244.4 0.5 copy.101
  244.9 0.7 fusion.15
  245.6 0.1 copy.103
  245.8 2.4 copy.102
  248.2 0.1 reduce_max.22
  248.2 1.5 fusion.11
  249.7 0.0 copy-start.4
  249.7 2.2 divide_convert_fusion
  251.9 0.0 copy-done.4
  251.9 0.0 copy-start
  252.0 1.7 fusion.4
  253.7 0.0 copy-done
  253.7 0.4 fusion.1
  254.1 0.1 copy.122
  254.3 1.1 reshape.82
  (3 shorter events, 0.1 us)
Async XLA Ops:
  7.2 28.0 %copy-start.6 = (f32[2,64,256]{2,1,0:T(8,128)S(1)}, f32[2,64,256]{2,1,0:T(8,128)}, u32[]{:S(2)}) copy-start(f32[2,64,256]{2,1,0:T(8,128)} %param.10) | copy-start | bytes 393220
  7.2 28.0 %copy-start.7 = (f32[2,64,256]{2,1,0:T(8,128)S(1)}, f32[2,64,256]{2,1,0:T(8,128)}, u32[]{:S(2)}) copy-start(f32[2,64,256]{2,1,0:T(8,128)} %param.11) | copy-start | bytes 393220
  7.2 28.0 %copy-start.5 = (f32[2,64,256]{2,1,0:T(8,128)S(1)}, f32[2,64,256]{2,1,0:T(8,128)}, u32[]{:S(2)}) copy-start(f32[2,64,256]{2,1,0:T(8,128)} %param.9) | copy-start | bytes 393220
  7.2 69.0 %all-gather.9.cloned.1.call-start = ((), (), s32[]{:S(2)}) async-start(), calls=%async_computation.2 | async-start | bytes 1179648 | tf_op jit(solution)/shard_map/all_gather | solution.py:42
  35.2 41.0 %copy-start.3 = (bf16[48,4,2048]{2,1,0:T(4,128)(2,1)S(1)}, bf16[48,4,2048]{2,1,0:T(4,128)(2,1)}, u32[]{:S(2)}) copy-start(bf16[48,4,2048]{2,1,0:T(4,128)(2,1)} %param.13) | copy-start | bytes 2359300
  39.9 36.8 %copy-start.1 = (bf16[48,24,2,256]{3,2,1,0:T(2,128)(2,1)S(1)}, bf16[48,24,2,256]{3,2,1,0:T(2,128)(2,1)}, u32[]{:S(2)}) copy-start(bf16[48,24,2,256]{3,2,1,0:T(2,128)(2,1)} %param.14) | copy-start | bytes 3538948
  39.9 79.5 %all-gather.7.cloned.1.call-start = ((), (), s32[]{:S(2)}) async-start(), calls=%async_computation.1 | async-start | bytes 3932160 | tf_op jit(solution)/shard_map/all_gather | solution.py:115
  40.7 177.5 %all-gather.11.cloned.1.call-start = ((), (), s32[]{:S(2)}) async-start(), calls=%async_computation.3 | async-start | bytes 9437184 | tf_op jit(solution)/shard_map/all_gather | solution.py:42
  81.6 1.9 copy-start.8
  226.5 8.4 %copy-start.2 = (bf16[192,8192,1]{1,0,2:T(8,128)(2,1)S(1)}, bf16[192,8192,1]{1,0,2:T(8,128)(2,1)}, u32[]{:S(2)}) copy-start(bf16[192,8192,1]{1,0,2:T(8,128)(2,1)} %reshape.77) | copy-start | bytes 9437188
  249.7 2.2 copy-start.4
  251.9 1.8 copy-start
Sparse Core Ops, SparseCore 0:
  40.0 36.0 all-gather.8
  78.3 41.1 all-gather.6
  121.5 96.6 all-gather.10
where the time goes:
time: 262 us
  waiting for transfers between devices  164 us (63%)
  local copies, waits for them, and re-layouts  35.6 us (14%)
  blocking collectives  30.5 us (12%)
  between operations  13.9 us (5%)
  matrix products  12.7 us (5%)
  other arithmetic  5.44 us (2%)
    all_gather x2, waiting for transfers between devices, all_blocks(): parts = lax.all_gather(parts, axes[k])  129 us
    all_gather x1, waiting for transfers between devices, on_device(): gathered = lax.all_gather(layer_inputs, 'tp', axis=2, tiled=True)  34.1 us
    all_to_all x1, blocking collectives, sent_and_summed(): parts = lax.all_to_all(split_up(x, dim, size), axis, 0, 0, tiled=True)  26.7 us
    transpose x1, local copies, waits for them, and re-layouts, in_order(): return jnp.moveaxis(parts, 0, dim).reshape(dims)  8.42 us
    transpose x1, local copies, waits for them, and re-layouts, all_blocks(): parts = parts.transpose(*back, *range(len(axes), parts.ndim))  8.26 us
    reshape x1, local copies, waits for them, and re-layouts, on_device(): flattened = gathered.reshape(row_count * step_count, gathered.shape[2])  5.5 us
    dot_general x1, matrix products, on_device(): jnp.einsum('td,kdc->ktc', flattened, whole_of(rollout_weight, REP_FSDP, (...  5.27 us
  transfers between devices with their start and end apart: 3, of which 3 were waited for; matrix products, arithmetic and copies ran while one was open for 6% of the time, Pallas kernels for 0%

commit v1 on v0

v1 whole, which is shorter than its diff:
```python
import jax
import jax.numpy as jnp
from jax import lax
from jax.experimental import pallas as pl
from jax.experimental.pallas import tpu as pltpu
from jax.sharding import Mesh
from jax.sharding import PartitionSpec as P

HD = 128
ROWS = 48
STEPS = 4
TOK = ROWS * STEPS
CACHE = 24
FEAT = 2048
COLS = 256
PACK = 4
GROUPS = ROWS // PACK
AXES = ("yh", "yl", "xl", "zh", "zl", "xh", "c")
SHARD = ("yh", "yl", "xl", "zh", "zl")
REP = ("yh", "yl", "xl")
FSDP = ("zh", "zl")
TP = ("xh", "c")
CUBE = ("yl", "xl", "zl")
FAR = ("yh", "zh")

beta_one = 0.9
beta_two = 0.95
learning_rate = 0.001
weight_decay = 0.1
epsilon = 1e-08
first_bias = 1.0 - 0.9**10
second_bias = 1.0 - 0.95**10


def adamw_update(gradient, master, moment_one, moment_two):
    new_one = beta_one * moment_one + (1.0 - beta_one) * gradient
    new_two = beta_two * moment_two + (1.0 - beta_two) * gradient * gradient
    update = new_one / first_bias / (jnp.sqrt(new_two / second_bias) + epsilon)
    new_master = master - learning_rate * (update + weight_decay * master)
    return (new_one, new_two, new_master)


def split_kernel(x_ref, o_ref):
    for b in range(4):
        v = [x_ref[:, b * 512 + 128 * k : b * 512 + 128 * (k + 1)] for k in range(4)]
        for half in range(2):
            cut = slice(64 * half, 64 * (half + 1))
            for p in range(2):
                o_ref[2 * b + half, :, 128 * p : 128 * (p + 1)] = jnp.concatenate(
                    [v[2 * p][:, cut], v[2 * p + 1][:, cut]], axis=1
                )


def split_features(x):
    return pl.pallas_call(
        split_kernel,
        out_shape=jax.ShapeDtypeStruct((8, TOK, COLS), jnp.bfloat16),
        grid=(1,),
        in_specs=[pl.BlockSpec((TOK, FEAT), lambda i: (0, 0))],
        out_specs=pl.BlockSpec((8, TOK, COLS), lambda i: (0, 0, 0)),
        name="split_features",
    )(x)


def project_kernel(x_ref, w_ref, o_ref):
    for kv in range(2):
        total = None
        for j in range(4):
            w = w_ref[4 * j : 4 * j + 4, kv].reshape(COLS, COLS)
            part = jnp.dot(x_ref[j, 0], w, preferred_element_type=jnp.float32)
            total = part if total is None else total + part
        o_ref[0, :, kv * COLS : (kv + 1) * COLS] = total.astype(jnp.bfloat16)


def project(x, w):
    return pl.pallas_call(
        project_kernel,
        out_shape=jax.ShapeDtypeStruct((8, TOK, 2 * COLS), jnp.bfloat16),
        grid=(8,),
        in_specs=[
            pl.BlockSpec((4, 1, TOK, COLS), lambda i: (0, i, 0, 0)),
            pl.BlockSpec((16, 2, 64, COLS), lambda i: (0, 0, 0, 0)),
        ],
        out_specs=pl.BlockSpec((1, TOK, 2 * COLS), lambda i: (i, 0, 0)),
        name="project",
    )(x, w)


def attend_kernel(per, part_ref, q_ref, k_ref, v_ref, mask_ref, o_ref):
    width = PACK * (CACHE + STEPS)
    old = PACK * CACHE
    new = PACK * STEPS
    row = lax.broadcasted_iota(jnp.int32, (8 * new, width), 0)
    col = lax.broadcasted_iota(jnp.int32, (8 * new, width), 1)
    own = (row // STEPS) % PACK
    own_col = jnp.where(col < old, col // CACHE, (col - old) // STEPS)
    seen = (own == own_col) & ((col < old) | ((col - old) % STEPS <= row % STEPS))
    for i in range(per):
        fresh = part_ref[0, new * i : new * (i + 1), :].astype(jnp.float32)
        for j in range(1, 8):
            fresh = fresh + part_ref[j, new * i : new * (i + 1), :].astype(jnp.float32)
        fresh = fresh.astype(jnp.bfloat16)
        valid = seen & (mask_ref[0, i : i + 1, :] > 0.0)
        for g in range(2):
            lanes = slice(HD * g, HD * (g + 1))
            q = jnp.concatenate(
                [
                    q_ref[new * i : new * (i + 1), HD * (8 * g + h) : HD * (8 * g + h + 1)]
                    for h in range(8)
                ],
                axis=0,
            )
            k = jnp.concatenate([k_ref[old * i : old * (i + 1), lanes], fresh[:, lanes]], axis=0)
            v = jnp.concatenate(
                [
                    v_ref[old * i : old * (i + 1), lanes],
                    fresh[:, COLS + HD * g : COLS + HD * (g + 1)],
                ],
                axis=0,
            )
            scores = lax.dot_general(
                q, k, (((1,), (1,)), ((), ())), preferred_element_type=jnp.float32
            )
            scores = jnp.where(valid, scores * (1.0 / HD**0.5), -jnp.inf)
            top = jnp.max(scores, axis=1, keepdims=True)
            e = jnp.exp(scores - top)
            weights = (e / jnp.sum(e, axis=1, keepdims=True)).astype(jnp.bfloat16)
            out = jnp.dot(weights, v, preferred_element_type=jnp.float32).astype(jnp.bfloat16)
            for h in range(8):
                o_ref[new * i : new * (i + 1), HD * (8 * g + h) : HD * (8 * g + h + 1)] = out[
                    new * h : new * (h + 1)
                ]


def attend(parts, q, keys, values, mask, blocks=4):
    per = GROUPS // blocks
    new = PACK * STEPS * per
    old = PACK * CACHE * per
    width = PACK * (CACHE + STEPS)

    def kernel(*refs):
        attend_kernel(per, *refs)

    return pl.pallas_call(
        kernel,
        out_shape=jax.ShapeDtypeStruct((TOK, FEAT), jnp.bfloat16),
        grid=(blocks,),
        in_specs=[
            pl.BlockSpec((8, new, 2 * COLS), lambda i: (0, i, 0)),
            pl.BlockSpec((new, FEAT), lambda i: (i, 0)),
            pl.BlockSpec((old, COLS), lambda i: (i, 0)),
            pl.BlockSpec((old, COLS), lambda i: (i, 0)),
            pl.BlockSpec((1, per, width), lambda i: (i, 0, 0)),
        ],
        out_specs=pl.BlockSpec((new, FEAT), lambda i: (i, 0)),
        name="attend",
    )(parts, q, keys, values, mask.reshape(blocks, per, width))


def on_device(
    grad_parts, master_weight, moment_one, moment_two, layer_inputs, queries, kv_cache, lengths
):
    pieces = jnp.moveaxis(grad_parts[0].reshape(2, 8, 64, COLS), 1, 0)
    pieces = lax.all_to_all(pieces, FSDP, 0, 0, tiled=True)
    gradient = jnp.sum(pieces.astype(jnp.float32), axis=0)
    new_one, new_two, new_master = adamw_update(gradient, master_weight, moment_one, moment_two)
    rollout = new_master.astype(jnp.bfloat16)

    features = split_features(layer_inputs.reshape(TOK, FEAT))
    features = lax.all_to_all(features, CUBE, 0, 0, tiled=True)
    features = lax.all_gather(features, TP)

    weight = jnp.broadcast_to(rollout[None], (16, 2, 64, COLS))
    weight = lax.all_to_all(weight, FAR, 0, 0, tiled=True)

    partial = project(features, weight)
    partial = lax.all_to_all(partial, CUBE, 0, 0, tiled=True)

    keys = kv_cache[:, :, 0].reshape(ROWS * CACHE, COLS)
    values = kv_cache[:, :, 1].reshape(ROWS * CACHE, COLS)
    cached = jnp.arange(CACHE, dtype=jnp.int32)[None, :] < lengths[:, None]
    mask = jnp.concatenate(
        [
            cached.reshape(GROUPS, PACK * CACHE).astype(jnp.float32),
            jnp.ones((GROUPS, PACK * STEPS), jnp.float32),
        ],
        axis=1,
    )
    context = attend(partial, queries.reshape(TOK, FEAT), keys, values, mask)
    return (new_master, new_one, new_two, context.reshape(ROWS, STEPS, FEAT))


def solution(mesh):
    finer = Mesh(mesh.devices.reshape(4, 2, 2, 4, 2, 2, 2), AXES)
    shard = P(None, SHARD, TP)
    return jax.shard_map(
        on_device,
        mesh=finer,
        in_specs=(
            P(FSDP, None, REP, TP),
            shard,
            shard,
            shard,
            P(SHARD, None, TP),
            P(SHARD, None, TP),
            P(SHARD, None, None, TP),
            P(SHARD),
        ),
        out_specs=(shard, shard, shard, P(SHARD, None, TP)),
        check_vma=False,
    )
```

time: 262 us -> 147 us (0.56)
  waiting for transfers between devices: 164 us -> 13.8 us
  blocking collectives: 30.5 us -> 77 us
  local copies, waits for them, and re-layouts: 35.6 us -> 11.9 us
  Pallas kernels: 0 us -> 18.7 us
  matrix products: 12.7 us -> 0 us
  starting transfers between devices: 0.12 us -> 9.8 us
  other arithmetic: 5.44 us -> 0.89 us
    all_gather x3 -> x1, waiting for transfers between devices: 163 us -> 0.01 us  [on_device(): features = lax.all_gather(features, TP)]
    all_to_all x1 -> x3, blocking collectives: 26.7 us -> 77 us  [the longest x1 36.2 us: on_device(): weight = lax.all_to_all(weight, FAR, 0, 0, tiled=True)]
    pallas_call x0 -> x3, Pallas kernels: none -> 18.7 us  [the longest x1 8.9 us: attend(): pl.pallas_call(kernel, out_shape=jax.ShapeDtypeStruct((TOK, FEAT), jnp.bf...]
    transpose x3 -> x1, local copies, waits for them, and re-layouts: 17.9 us -> 0.04 us  [on_device(): pieces = jnp.moveaxis(grad_parts[0].reshape(2, 8, 64, COLS), 1, 0)]
    all_to_all x0 -> x1, waiting for transfers between devices: none -> 13.8 us  [on_device(): partial = lax.all_to_all(partial, CUBE, 0, 0, tiled=True)]
    dot_general x5 -> x0, matrix products: 12.7 us -> none  [the longest x1 5.27 us: on_device(): jnp.einsum('td,kdc->ktc', flattened, whole_of(rollout_weight, REP_FSDP, (...]
    all_to_all x0 -> x1, starting transfers between devices: none -> 9.76 us  [on_device(): partial = lax.all_to_all(partial, CUBE, 0, 0, tiled=True)]
    slice x2 -> x1, local copies, waits for them, and re-layouts: 5.55 us -> 1.63 us  [on_device(): values = kv_cache[:, :, 1].reshape(ROWS * CACHE, COLS)]
  transfers between devices with their start and end apart: 3 -> 2, of which waited for: 3 -> 1; matrix products, arithmetic and copies ran while one was open for 6% -> 4% of each run, Pallas kernels for 0% -> 0%
where the time goes in v1:
time: 147 us; the launch traced here: 146 us
  blocking collectives  77 us (52%)
  Pallas kernels  18.7 us (13%)
  between operations  14.1 us (10%)
  waiting for transfers between devices  13.8 us (9%)
  local copies, waits for them, and re-layouts  11.9 us (8%)
  starting transfers between devices  9.8 us (7%)
    all_to_all x1, blocking collectives, on_device(): weight = lax.all_to_all(weight, FAR, 0, 0, tiled=True)  36.2 us
    all_to_all x1, blocking collectives, on_device(): pieces = lax.all_to_all(pieces, FSDP, 0, 0, tiled=True)  26.1 us
    all_to_all x1, blocking collectives, on_device(): features = lax.all_to_all(features, CUBE, 0, 0, tiled=True)  14.8 us
    all_to_all x1, waiting for transfers between devices, on_device(): partial = lax.all_to_all(partial, CUBE, 0, 0, tiled=True)  13.8 us
    all_to_all x1, starting transfers between devices, on_device(): partial = lax.all_to_all(partial, CUBE, 0, 0, tiled=True)  9.76 us
    pallas_call x1, Pallas kernels, attend(): pl.pallas_call(kernel, out_shape=jax.ShapeDtypeStruct((TOK, FEAT), jnp.bf...  8.9 us
    pallas_call x1, Pallas kernels, project(): pl.pallas_call(project_kernel, out_shape=jax.ShapeDtypeStruct((8, TOK, 2...  7.49 us
    unnamed x18, local copies, waits for them, and re-layouts  3.53 us
  transfers between devices with their start and end apart: 2, of which 1 were waited for; matrix products, arithmetic and copies ran while one was open for 4% of the time, Pallas kernels for 0%

profile of v1, /device:TPU:1, one launch (start us, length us, event | category | flops | bytes accessed | tf_op | source)
XLA Modules:
  0.0 146.2 jit_solution(4677315748958762849)
XLA Ops:
  7.2 0.0 all-gather.3.cloned.1.call-start
  7.2 2.3 %reshape.29.x_ref = bf16[192,2048]{1,0:T(8,128)(2,1)} reshape(bf16[48,4,2048]{2,1,0:T(4,128)(2,1)} %param.12) | data formatting | bytes 1572864 | tf_op jit(solution)/shard_map/reshape | solution.py:169
  9.5 2.3 %split_features.1 = bf16[8,192,256]{2,1,0:T(8,128)(2,1)} custom-call(bf16[192,2048]{1,0:T(8,128)(2,1)} %reshape.29.x_ref), custom_call_target="tpu_custom_call" | custom-call | tf_op jit(solution)/shard_map/split_features/pallas_call | solution.py:55
  11.8 0.0 copy-start.3
  11.8 14.8 %all_to_all.20 = bf16[8,192,256]{2,1,0:T(8,128)(2,1)} all-to-all(bf16[8,192,256]{2,1,0:T(8,128)(2,1)} %split_features.1), channel_id=1, replica_groups=mesh['yh'=4,'yl'=2,'xl'=2,'zh'=4,'zl'=2,'xh'=2,'c'=2] {'yl','xl','zl'}, dimensions={0} | all-to-all | bytes 1572864 | tf_op jit(solution)/shard_map/all_to_all | solution.py:170
  26.5 0.0 all-gather.3.cloned.1.call-update
  26.5 0.0 copy-done.3
  26.6 0.0 copy-start.4
  26.6 0.0 copy-start.5
  26.6 0.0 copy-start.6
  26.6 26.1 %all_to_all.21 = bf16[8,2,64,256]{3,2,1,0:T(8,128)(2,1)S(1)} all-to-all(bf16[8,2,64,256]{3,2,1,0:T(8,128)(2,1)S(1)} %copy.16), channel_id=1, replica_groups=mesh['yh'=4,'yl'=2,'xl'=2,'zh'=4,'zl'=2,'xh'=2,'c'=2] {'zh','zl'}, dimensions={0} | all-to-all | bytes 1048576 | tf_op jit(solution)/shard_map/all_to_all | solution.py:164
  52.7 0.1 convert_reduce_fusion
  52.8 0.0 copy-done.4
  52.8 0.0 copy-done.5
  52.8 0.0 copy-done.6
  52.8 0.8 fusion.1
  53.6 0.1 broadcast_in_dim.2
  53.7 36.2 %all_to_all.22.w_ref = bf16[16,2,64,256]{3,2,1,0:T(8,128)(2,1)} all-to-all(bf16[16,2,64,256]{3,2,1,0:T(8,128)(2,1)S(1)} %broadcast_in_dim.2), channel_id=1, replica_groups=mesh['yh'=4,'yl'=2,'xl'=2,'zh'=4,'zl'=2,'xh'=2,'c'=2] {'yh','zh'}, dimensions={0} | all-to-all | bytes 2097152 | tf_op jit(solution)/shard_map/all_to_all | solution.py:174
  89.9 0.0 all-gather.3.cloned.1.call-done
  89.9 7.5 %project.1 = bf16[8,192,512]{2,1,0:T(8,128)(2,1)} custom-call(bf16[4,8,192,256]{3,2,1,0:T(8,128)(2,1)} %bitcast.6, bf16[16,2,64,256]{3,2,1,0:T(8,128)(2,1)} %all_to_all.22.w_ref), custom_call_target="tpu_custom_call" | custom-call | tf_op jit(solution)/shard_map/project/pallas_call | solution.py:76
  97.4 0.0 copy-start.2
  97.4 9.8 %all-to-all-start.3 = ((bf16[8,192,512]{2,1,0:T(8,128)(2,1)}), bf16[8,192,512]{2,1,0:T(8,128)(2,1)S(1)}, u32[]{:S(2)}, u32[]{:S(2)}) async-start(bf16[8,192,512]{2,1,0:T(8,128)(2,1)} %project.1), calls=%async_computation.3 | async-start | bytes 3145728 | tf_op jit(solution)/shard_map/all_to_all | solution.py:177
  107.2 0.0 copy-done.2
  107.2 0.0 copy-start.1
  107.2 1.1 reshape.30.refs_1_
  108.3 0.5 copy-done.1
  108.7 1.6 %fusion.3 = (bf16[48,24,1,256]{3,2,1,0:T(2,128)(2,1)S(1)}, bf16[48,24,1,256]{3,2,1,0:T(2,128)(2,1)S(1)}) fusion(bf16[48,24,2,256]{3,2,1,0:T(2,128)(2,1)S(1)} %copy-done.1), kind=kLoop, calls=%fused_computation.8 | loop fusion | bytes 2359296 | tf_op jit(solution)/shard_map/slice | solution.py:180
  110.4 0.9 copy.19
  111.3 0.0 copy-start.7
  111.3 0.9 copy.20
  112.2 0.0 copy-done.7
  112.2 0.1 lt.25
  112.3 0.1 lt.26
  112.4 0.1 lt.27
  112.5 0.1 lt.23
  112.6 0.6 reshape.35.refs_4_
  113.2 13.8 %all-to-all-done.3.refs_0_ = bf16[8,192,512]{2,1,0:T(8,128)(2,1)S(1)} async-done(((bf16[8,192,512]{2,1,0:T(8,128)(2,1)}), bf16[8,192,512]{2,1,0:T(8,128)(2,1)S(1)}, u32[]{:S(2)}, u32[]{:S(2)}) %all-to-all-start.3) | async-done | bytes 1572896 | tf_op jit(solution)/shard_map/all_to_all | solution.py:177
  127.0 0.0 copy-start
  127.0 1.2 copy-done
  128.1 8.9 %attend.1 = bf16[192,2048]{1,0:T(8,128)(2,1)} custom-call(bf16[8,192,512]{2,1,0:T(8,128)(2,1)} %copy-done, bf16[192,2048]{1,0:T(8,128)(2,1)} %reshape.30.refs_1_, bf16[1152,256]{1,0:T(8,128)(2,1)} %bitcast.7, bf16[1152,256]{1,0:T(8,128)(2,1)} %bitcast.8, f32[4,3,112]{2,1,0:T(4,128)} %reshape.35.refs_4_), custom_call_target="tpu_custom_call" | custom-call | tf_op jit(solution)/shard_map/attend/pallas_call | solution.py:144
  137.0 2.4 %reshape.33 = bf16[48,4,2048]{2,1,0:T(4,128)(2,1)} reshape(bf16[192,2048]{1,0:T(8,128)(2,1)} %attend.1) | data formatting | bytes 1572864 | tf_op jit(solution)/shard_map/reshape | solution.py:190
  (4 shorter events, 0.1 us)
Async XLA Ops:
  7.2 82.8 %all-gather.3.cloned.1.call-start = ((), (), s32[]{:S(2)}) async-start(), calls=%async_computation.4 | async-start | bytes 3932160 | tf_op jit(solution)/shard_map/all_gather | solution.py:171
  11.8 14.8 %copy-start.3 = (bf16[1,2,512,256]{3,2,1,0:T(8,128)(2,1)S(1)}, bf16[1,2,512,256]{3,2,1,0:T(8,128)(2,1)}, u32[]{:S(2)}) copy-start(bf16[1,2,512,256]{3,2,1,0:T(8,128)(2,1)} %param.8) | copy-start | bytes 1572868
  26.6 26.2 %copy-start.4 = (f32[2,64,256]{2,1,0:T(8,128)S(1)}, f32[2,64,256]{2,1,0:T(8,128)}, u32[]{:S(2)}) copy-start(f32[2,64,256]{2,1,0:T(8,128)} %param.9) | copy-start | bytes 393220
  26.6 26.2 %copy-start.5 = (f32[2,64,256]{2,1,0:T(8,128)S(1)}, f32[2,64,256]{2,1,0:T(8,128)}, u32[]{:S(2)}) copy-start(f32[2,64,256]{2,1,0:T(8,128)} %param.10) | copy-start | bytes 393220
  26.6 26.2 %copy-start.6 = (f32[2,64,256]{2,1,0:T(8,128)S(1)}, f32[2,64,256]{2,1,0:T(8,128)}, u32[]{:S(2)}) copy-start(f32[2,64,256]{2,1,0:T(8,128)} %param.11) | copy-start | bytes 393220
  97.4 9.8 %copy-start.2 = (bf16[48,4,2048]{2,1,0:T(4,128)(2,1)S(1)}, bf16[48,4,2048]{2,1,0:T(4,128)(2,1)}, u32[]{:S(2)}) copy-start(bf16[48,4,2048]{2,1,0:T(4,128)(2,1)} %param.13) | copy-start | bytes 2359300
  97.4 29.5 %all-to-all-start.3 = ((bf16[8,192,512]{2,1,0:T(8,128)(2,1)}), bf16[8,192,512]{2,1,0:T(8,128)(2,1)S(1)}, u32[]{:S(2)}, u32[]{:S(2)}) async-start(bf16[8,192,512]{2,1,0:T(8,128)(2,1)} %project.1), calls=%async_computation.3 | async-start | bytes 3145728 | tf_op jit(solution)/shard_map/all_to_all | solution.py:177
  107.2 1.6 %copy-start.1 = (bf16[48,24,2,256]{3,2,1,0:T(2,128)(2,1)S(1)}, bf16[48,24,2,256]{3,2,1,0:T(2,128)(2,1)}, u32[]{:S(2)}) copy-start(bf16[48,24,2,256]{3,2,1,0:T(2,128)(2,1)} %param.14) | copy-start | bytes 3538948
  111.3 0.9 copy-start.7
  127.0 1.2 copy-start
Sparse Core Ops, SparseCore 0:
  26.7 45.8 all-gather.2

commit v2 on v1

v2 whole, which is shorter than its diff:
```python
import jax
import jax.numpy as jnp
from jax import lax
from jax.experimental import pallas as pl
from jax.experimental.pallas import tpu as pltpu
from jax.sharding import Mesh
from jax.sharding import PartitionSpec as P

HD = 128
ROWS = 48
STEPS = 4
TOK = ROWS * STEPS
CACHE = 24
FEAT = 2048
COLS = 256
PACK = 4
GROUPS = ROWS // PACK
AXES = ("yh", "yl", "xl", "zh", "zl", "xh", "c")
SHARD = ("yh", "yl", "xl", "zh", "zl")
REP = ("yh", "yl", "xl")
FSDP = ("zh", "zl")
TP = ("xh", "c")
CUBE = ("yl", "xl", "zl")
FAR = ("yh", "zh")

beta_one = 0.9
beta_two = 0.95
learning_rate = 0.001
weight_decay = 0.1
epsilon = 1e-08
first_bias = 1.0 - 0.9**10
second_bias = 1.0 - 0.95**10


def adamw_update(gradient, master, moment_one, moment_two):
    new_one = beta_one * moment_one + (1.0 - beta_one) * gradient
    new_two = beta_two * moment_two + (1.0 - beta_two) * gradient * gradient
    update = new_one / first_bias / (jnp.sqrt(new_two / second_bias) + epsilon)
    new_master = master - learning_rate * (update + weight_decay * master)
    return (new_one, new_two, new_master)


VM = pl.BlockSpec(memory_space=pltpu.VMEM)
SM = pl.BlockSpec(memory_space=pltpu.SMEM)
PARAMS = pltpu.CompilerParams(vmem_limit_bytes=40 << 20)


def split_kernel(x_ref, o_ref):
    for b in range(4):
        v = [
            x_ref[:, :, 512 * b + 128 * k : 512 * b + 128 * (k + 1)].reshape(TOK, 128)
            for k in range(4)
        ]
        for half in range(2):
            cut = slice(64 * half, 64 * (half + 1))
            for p in range(2):
                o_ref[2 * b + half, :, 128 * p : 128 * (p + 1)] = jnp.concatenate(
                    [v[2 * p][:, cut], v[2 * p + 1][:, cut]], axis=1
                )


def split_features(x):
    return pl.pallas_call(
        split_kernel,
        out_shape=jax.ShapeDtypeStruct((8, TOK, COLS), jnp.bfloat16),
        in_specs=[VM],
        out_specs=VM,
        compiler_params=PARAMS,
        name="split_features",
    )(x)


def project_kernel(t_ref, xa, xb, xc, xd, w_ref, o_ref):
    own = t_ref[0]
    for kv in range(2):
        w = jnp.concatenate(
            [w_ref[pl.ds(4 * (own ^ f), 4), kv].reshape(COLS, COLS) for f in range(4)], axis=0
        )
        for m in range(0, 8, 2):
            x = jnp.concatenate(
                [r[m : m + 2].reshape(2 * TOK, COLS) for r in (xa, xb, xc, xd)], axis=1
            )
            y = jnp.dot(x, w, preferred_element_type=jnp.float32).astype(jnp.bfloat16)
            o_ref[m : m + 2, :, kv * COLS : (kv + 1) * COLS] = y.reshape(2, TOK, COLS)


def project(own, features, w):
    return pl.pallas_call(
        project_kernel,
        out_shape=jax.ShapeDtypeStruct((8, TOK, 2 * COLS), jnp.bfloat16),
        in_specs=[SM] + [VM] * 5,
        out_specs=VM,
        compiler_params=PARAMS,
        name="project",
    )(own, *features, w)


def seen_bias(axis):
    width, old, count = PACK * (CACHE + STEPS), PACK * CACHE, 8 * PACK * STEPS
    shape = (count, width) if axis == 1 else (width, count)
    row = lax.broadcasted_iota(jnp.int32, shape, 1 - axis)
    col = lax.broadcasted_iota(jnp.int32, shape, axis)
    own = (row // STEPS) % PACK
    of_col = jnp.where(col < old, col // CACHE, (col - old) // STEPS)
    seen = (own == of_col) & ((col < old) | ((col - old) % STEPS <= row % STEPS))
    return jnp.where(seen, 0.0, -jnp.inf)


def attend_kernel(part_ref, q_ref, k_ref, v_ref, mask_ref, mask_t_ref, o_ref):
    old, new = PACK * CACHE, PACK * STEPS
    width, count = old + new, 8 * new
    scale = 1.4426950408889634 / HD**0.5
    base, base_t = seen_bias(1), seen_bias(0)
    eye = lax.broadcasted_iota(jnp.int32, (count, count), 0) == lax.broadcasted_iota(
        jnp.int32, (count, count), 1
    )
    minus = jnp.full((width, count), -1.0, jnp.bfloat16)
    ones = jnp.ones((width, HD), jnp.bfloat16)
    for i in range(GROUPS):
        rows = slice(PACK * i, PACK * (i + 1))
        fresh = part_ref[0, new * i : new * (i + 1), :].astype(jnp.float32)
        for j in range(1, 8):
            fresh = fresh + part_ref[j, new * i : new * (i + 1), :].astype(jnp.float32)
        fresh = fresh.astype(jnp.bfloat16)
        bias = base + mask_ref[i : i + 1, :]
        bias_t = base_t + mask_t_ref[:, i : i + 1]
        for g in range(2):
            lanes = slice(HD * g, HD * (g + 1))
            heads = [slice(HD * (8 * g + h), HD * (8 * g + h + 1)) for h in range(8)]
            q = jnp.concatenate([q_ref[rows, :, h].reshape(new, HD) for h in heads], axis=0)
            k = jnp.concatenate([k_ref[old * i : old * (i + 1), lanes], fresh[:, lanes]], axis=0)
            v = jnp.concatenate(
                [
                    v_ref[old * i : old * (i + 1), lanes],
                    fresh[:, COLS + HD * g : COLS + HD * (g + 1)],
                ],
                axis=0,
            )
            turned = lax.dot_general(
                k, q, (((1,), (1,)), ((), ())), preferred_element_type=jnp.float32
            )
            top = jnp.max(turned + bias_t, axis=0, keepdims=True)
            shift = jnp.where(eye, top, 0.0).astype(jnp.bfloat16)
            scores = lax.dot_general(
                jnp.concatenate([q, shift], axis=1),
                jnp.concatenate([k, minus], axis=1),
                (((1,), (1,)), ((), ())),
                preferred_element_type=jnp.float32,
            )
            e = jnp.exp2(scores * scale + bias).astype(jnp.bfloat16)
            out = jnp.dot(
                e, jnp.concatenate([v, ones], axis=1), preferred_element_type=jnp.float32
            )
            out = (out[:, :HD] / out[:, HD:]).astype(jnp.bfloat16)
            for n, h in enumerate(heads):
                o_ref[rows, :, h] = out[new * n : new * (n + 1)].reshape(PACK, STEPS, HD)


def attend(parts, q, keys, values, mask):
    return pl.pallas_call(
        attend_kernel,
        out_shape=jax.ShapeDtypeStruct((ROWS, STEPS, FEAT), jnp.bfloat16),
        in_specs=[VM] * 6,
        out_specs=VM,
        compiler_params=PARAMS,
        name="attend",
    )(parts, q, keys, values, mask, mask.T)


def flipped(x, axis):
    return lax.ppermute(x, axis, [(0, 1), (1, 0)])


def on_device(
    grad_parts, master_weight, moment_one, moment_two, layer_inputs, queries, kv_cache, lengths
):
    pieces = jnp.moveaxis(grad_parts[0].reshape(2, 8, 64, COLS), 1, 0)
    pieces = lax.all_to_all(pieces, FSDP, 0, 0, tiled=True)
    gradient = jnp.sum(pieces.astype(jnp.float32), axis=0)
    new_one, new_two, new_master = adamw_update(gradient, master_weight, moment_one, moment_two)
    rollout = new_master.astype(jnp.bfloat16)

    features = split_features(layer_inputs)
    features = lax.all_to_all(features, CUBE, 0, 0, tiled=True)
    beside = flipped(features, "c")
    across = flipped(features, "xh")
    beyond = flipped(across, "c")

    weight = jnp.broadcast_to(rollout[None], (16, 2, 64, COLS))
    weight = lax.all_to_all(weight, FAR, 0, 0, tiled=True)

    own = (lax.axis_index("xh") * 2 + lax.axis_index("c")).astype(jnp.int32).reshape(1)
    partial = project(own, (features, beside, across, beyond), weight)
    partial = lax.all_to_all(partial, CUBE, 0, 0, tiled=True)

    keys = kv_cache[:, :, 0].reshape(ROWS * CACHE, COLS)
    values = kv_cache[:, :, 1].reshape(ROWS * CACHE, COLS)
    cached = jnp.arange(CACHE, dtype=jnp.int32)[None, :] < lengths[:, None]
    mask = jnp.concatenate(
        [
            jnp.where(cached, 0.0, -jnp.inf).reshape(GROUPS, PACK * CACHE),
            jnp.zeros((GROUPS, PACK * STEPS), jnp.float32),
        ],
        axis=1,
    )
    context = attend(partial, queries, keys, values, mask)
    return (new_master, new_one, new_two, context)


def solution(mesh):
    finer = Mesh(mesh.devices.reshape(4, 2, 2, 4, 2, 2, 2), AXES)
    shard = P(None, SHARD, TP)
    return jax.shard_map(
        on_device,
        mesh=finer,
        in_specs=(
            P(FSDP, None, REP, TP),
            shard,
            shard,
            shard,
            P(SHARD, None, TP),
            P(SHARD, None, TP),
            P(SHARD, None, None, TP),
            P(SHARD),
        ),
        out_specs=(shard, shard, shard, P(SHARD, None, TP)),
        check_vma=False,
    )
```

time: 147 us -> 125 us (0.85)
  blocking collectives: 77 us -> 0 us
  starting transfers between devices: 9.8 us -> 48.8 us
  waiting for transfers between devices: 13.8 us -> 52.8 us
  between operations: 14.1 us -> 0.79 us
  Pallas kernels: 18.7 us -> 11.1 us
  local copies, waits for them, and re-layouts: 11.9 us -> 8.84 us
    all_to_all x3 -> x0, blocking collectives: 77 us -> none  [the longest x1 36.2 us: on_device(): weight = lax.all_to_all(weight, FAR, 0, 0, tiled=True)]
    all_to_all x0 -> x3, waiting for transfers between devices: none -> 25.9 us  [the longest x1 16.7 us: on_device(): pieces = lax.all_to_all(pieces, FSDP, 0, 0, tiled=True)]
    all_to_all x0 -> x3, starting transfers between devices: none -> 21.7 us  [the longest x1 10.9 us: on_device(): pieces = lax.all_to_all(pieces, FSDP, 0, 0, tiled=True)]
    ppermute x0 -> x3, starting transfers between devices: none -> 14.4 us  [flipped(): return lax.ppermute(x, axis, [(0, 1), (1, 0)])]
    ppermute x0 -> x3, waiting for transfers between devices: none -> 12.8 us  [flipped(): return lax.ppermute(x, axis, [(0, 1), (1, 0)])]
    reshape x4 -> x0, local copies, waits for them, and re-layouts: 6.29 us -> none  [the longest x1 2.37 us: on_device(): return (new_master, new_one, new_two, context.reshape(ROWS, STEPS, FEAT))]
    pallas_call x1, Pallas kernels: 7.49 us -> 4.09 us  [project(): pl.pallas_call(project_kernel, out_shape=jax.ShapeDtypeStruct((8, TOK, 2...]
    pallas_call x1, Pallas kernels: 8.9 us -> 5.71 us  [attend(): pl.pallas_call(attend_kernel, out_shape=jax.ShapeDtypeStruct((ROWS, STEPS...]
  transfers between devices with their start and end apart: 2 -> 7, of which waited for: 1 -> 5; matrix products, arithmetic and copies ran while one was open for 4% -> 5% of each run, Pallas kernels for 0% -> 1%
where the time goes in v2:
time: 125 us; the launch traced here: 124 us
  waiting for transfers between devices  52.8 us (42%)
  starting transfers between devices  48.8 us (39%)
  Pallas kernels  11.1 us (9%)
  local copies, waits for them, and re-layouts  8.84 us (7%)
  other arithmetic  1.57 us (1%)
    all_to_all x1, waiting for transfers between devices, on_device(): pieces = lax.all_to_all(pieces, FSDP, 0, 0, tiled=True)  16.7 us
    ppermute x3, starting transfers between devices, flipped(): return lax.ppermute(x, axis, [(0, 1), (1, 0)])  14.4 us
    all_to_all x1, waiting for transfers between devices, on_device(): partial = lax.all_to_all(partial, CUBE, 0, 0, tiled=True)  14.1 us
    ppermute x3, waiting for transfers between devices, flipped(): return lax.ppermute(x, axis, [(0, 1), (1, 0)])  12.8 us
    all_to_all x1, starting transfers between devices, on_device(): partial = lax.all_to_all(partial, CUBE, 0, 0, tiled=True)  12.7 us
    all_to_all x1, starting transfers between devices, on_device(): pieces = lax.all_to_all(pieces, FSDP, 0, 0, tiled=True)  10.9 us
    all_to_all x1, waiting for transfers between devices, on_device(): features = lax.all_to_all(features, CUBE, 0, 0, tiled=True)  9.2 us
    all_to_all x1, starting transfers between devices, on_device(): weight = lax.all_to_all(weight, FAR, 0, 0, tiled=True)  7.3 us
  transfers between devices with their start and end apart: 7, of which 5 were waited for; matrix products, arithmetic and copies ran while one was open for 5% of the time, Pallas kernels for 1%

profile of v2, /device:TPU:1, one launch (start us, length us, event | category | flops | bytes accessed | tf_op | source)
XLA Modules:
  0.0 123.9 jit_solution(4844526560442126771)
XLA Ops:
  0.6 0.0 copy-start
  0.6 2.0 %copy.22 = bf16[8,2,64,256]{3,2,1,0:T(8,128)(2,1)} copy(bf16[8,2,64,256]{3,2,0,1:T(8,128)(2,1)} %bitcast.14) | data formatting | bytes 1048576 | tf_op jit(solution)/shard_map/transpose | solution.py:177
  2.6 10.9 %all-to-all-start = ((bf16[8,2,64,256]{3,2,1,0:T(8,128)(2,1)}), bf16[8,2,64,256]{3,2,1,0:T(8,128)(2,1)S(1)}, u32[]{:S(2)}, u32[]{:S(2)}) async-start(bf16[8,2,64,256]{3,2,1,0:T(8,128)(2,1)} %copy.22), calls=%async_computation | async-start | bytes 1048576 | tf_op jit(solution)/shard_map/all_to_all | solution.py:178
  13.5 0.0 copy-done
  13.5 1.3 %split_features.1 = bf16[8,192,256]{2,1,0:T(8,128)(2,1)} custom-call(bf16[48,4,2048]{2,1,0:T(4,128)(2,1)S(1)} %copy-done), custom_call_target="tpu_custom_call" | custom-call | tf_op jit(solution)/shard_map/split_features/pallas_call | solution.py:63
  14.7 0.0 copy-start.4
  14.7 0.0 copy-start.5
  14.7 0.0 copy-start.6
  14.7 16.7 %all-to-all-done = bf16[8,2,64,256]{3,2,1,0:T(8,128)(2,1)S(1)} async-done(((bf16[8,2,64,256]{3,2,1,0:T(8,128)(2,1)}), bf16[8,2,64,256]{3,2,1,0:T(8,128)(2,1)S(1)}, u32[]{:S(2)}, u32[]{:S(2)}) %all-to-all-start) | async-done | bytes 524320 | tf_op jit(solution)/shard_map/all_to_all | solution.py:178
  31.4 3.5 %all-to-all-start.1 = ((bf16[8,192,256]{2,1,0:T(8,128)(2,1)}), bf16[8,192,256]{2,1,0:T(8,128)(2,1)S(1)}, u32[]{:S(2)}, u32[]{:S(2)}) async-start(bf16[8,192,256]{2,1,0:T(8,128)(2,1)} %split_features.1), calls=%async_computation.1 | async-start | bytes 1572864 | tf_op jit(solution)/shard_map/all_to_all | solution.py:184
  35.0 0.1 convert_reduce_fusion
  35.1 0.0 copy-done.4
  35.1 0.0 copy-done.5
  35.1 0.0 copy-done.6
  35.1 0.8 fusion.2
  35.9 9.2 %all-to-all-done.1.xa = bf16[8,192,256]{2,1,0:T(8,128)(2,1)S(1)} async-done(((bf16[8,192,256]{2,1,0:T(8,128)(2,1)}), bf16[8,192,256]{2,1,0:T(8,128)(2,1)S(1)}, u32[]{:S(2)}, u32[]{:S(2)}) %all-to-all-start.1) | async-done | bytes 786464 | tf_op jit(solution)/shard_map/all_to_all | solution.py:184
  45.1 1.1 broadcast_in_dim.8
  46.2 7.3 %all-to-all-start.2 = ((bf16[16,2,64,256]{3,2,1,0:T(8,128)(2,1)}), bf16[16,2,64,256]{3,2,1,0:T(8,128)(2,1)S(1)}, u32[]{:S(2)}, u32[]{:S(2)}) async-start(bf16[16,2,64,256]{3,2,1,0:T(8,128)(2,1)} %broadcast_in_dim.8), calls=%async_computation.2 | async-start | bytes 2097152 | tf_op jit(solution)/shard_map/all_to_all | solution.py:190
  53.5 4.7 %collective-permute-start.1 = (bf16[8,192,256]{2,1,0:T(8,128)(2,1)S(1)}, bf16[8,192,256]{2,1,0:T(8,128)(2,1)S(1)}, u32[]{:S(2)}, u32[]{:S(2)}) collective-permute-start(bf16[8,192,256]{2,1,0:T(8,128)(2,1)S(1)} %all-to-all-done.1.xa), channel_id=1, source_target_pairs={{0,2},{2,0},{1,3},{3,1},{4,6},{6,4},{5,7},{7,5},{8,10},{10,8},{9,1... | collective-permute-start | bytes 2359304 | tf_op jit(solution)/shard_map/ppermute | solution.py:171
  58.2 4.6 %collective-permute-start = (bf16[8,192,256]{2,1,0:T(8,128)(2,1)S(1)}, bf16[8,192,256]{2,1,0:T(8,128)(2,1)S(1)}, u32[]{:S(2)}, u32[]{:S(2)}) collective-permute-start(bf16[8,192,256]{2,1,0:T(8,128)(2,1)S(1)} %all-to-all-done.1.xa), channel_id=1, source_target_pairs={{0,1},{1,0},{2,3},{3,2},{4,5},{5,4},{6,7},{7,6},{8,9},{9,8},{10,11... | collective-permute-start | bytes 2359304 | tf_op jit(solution)/shard_map/ppermute | solution.py:171
  62.7 10.8 %collective-permute-done.1.xc = bf16[8,192,256]{2,1,0:T(8,128)(2,1)S(1)} collective-permute-done((bf16[8,192,256]{2,1,0:T(8,128)(2,1)S(1)}, bf16[8,192,256]{2,1,0:T(8,128)(2,1)S(1)}, u32[]{:S(2)}, u32[]{:S(2)}) %collective-permute-start.1) | collective-permute-done | bytes 786464 | tf_op jit(solution)/shard_map/ppermute | solution.py:171
  73.5 5.2 %collective-permute-start.2 = (bf16[8,192,256]{2,1,0:T(8,128)(2,1)S(1)}, bf16[8,192,256]{2,1,0:T(8,128)(2,1)}, u32[]{:S(2)}, u32[]{:S(2)}) collective-permute-start(bf16[8,192,256]{2,1,0:T(8,128)(2,1)S(1)} %collective-permute-done.1.xc), channel_id=1, source_target_pairs={{0,1},{1,0},{2,3},{3,2},{4,5},{5,4},{6,7},{7,6},{8,9},{9,8},{10,11... | collective-permute-start | bytes 2359304 | tf_op jit(solution)/shard_map/ppermute | solution.py:171
  78.8 0.0 collective-permute-done.xb
  78.8 0.0 all-to-all-done.2.w_ref
  78.8 2.0 %collective-permute-done.2.xd = bf16[8,192,256]{2,1,0:T(8,128)(2,1)} collective-permute-done((bf16[8,192,256]{2,1,0:T(8,128)(2,1)S(1)}, bf16[8,192,256]{2,1,0:T(8,128)(2,1)}, u32[]{:S(2)}, u32[]{:S(2)}) %collective-permute-start.2) | collective-permute-done | bytes 786464 | tf_op jit(solution)/shard_map/ppermute | solution.py:171
  80.8 4.1 %project.1 = bf16[8,192,512]{2,1,0:T(8,128)(2,1)} custom-call(s32[1]{0:T(128)} %bitcast.2.t_ref, bf16[8,192,256]{2,1,0:T(8,128)(2,1)S(1)} %all-to-all-done.1.xa, bf16[8,192,256]{2,1,0:T(8,128)(2,1)S(1)} %collective-permute-done.xb, bf16[8,192,256]{2,1,0:T(8,128)(2,1)S(1)} %collective-permute-done.1.xc, bf16[8,192,256]{2,1,0:T(8,128)(2,1)} %collective-permute-done.2.xd, ...), custom_call_target="tpu_custom_call" | custom-call | tf_op jit(solution)/shard_map/project/pallas_call | solution.py:88
  84.9 0.0 copy-start.3
  84.9 12.7 %all-to-all-start.3 = ((bf16[8,192,512]{2,1,0:T(8,128)(2,1)}), bf16[8,192,512]{2,1,0:T(8,128)(2,1)S(1)}, u32[]{:S(2)}, u32[]{:S(2)}) async-start(bf16[8,192,512]{2,1,0:T(8,128)(2,1)} %project.1), calls=%async_computation.3 | async-start | bytes 3145728 | tf_op jit(solution)/shard_map/all_to_all | solution.py:194
  97.6 0.0 copy-done.3
  97.6 1.6 %fusion.4 = (bf16[48,24,1,256]{3,2,1,0:T(2,128)(2,1)S(1)}, bf16[48,24,1,256]{3,2,1,0:T(2,128)(2,1)S(1)}) fusion(bf16[48,24,2,256]{3,2,1,0:T(2,128)(2,1)S(1)} %copy-done.3), kind=kLoop, calls=%fused_computation.9 | loop fusion | bytes 2359296 | tf_op jit(solution)/shard_map/slice | solution.py:197
  99.2 0.1 copy.27
  99.3 0.0 copy-start.7
  99.3 0.0 copy-start.1
  99.4 0.1 copy.28
  99.5 0.5 copy-done.7
  100.0 0.1 lt.25
  100.1 0.1 copy.25
  100.2 0.1 lt.23
  100.3 0.7 fusion.1
  101.0 0.9 copy.29
  101.8 1.4 %pad_bitcast_fusion.mask_t_ref = f32[112,12]{1,0:T(8,128)} fusion(f32[12,96]{0,1:T(8,128)} %fusion.1), kind=kLoop, calls=%fused_computation.7 | loop fusion | bytes 9984 | tf_op jit(solution)/shard_map/transpose | solution.py:167
  103.3 14.1 %all-to-all-done.3.part_ref = bf16[8,192,512]{2,1,0:T(8,128)(2,1)S(1)} async-done(((bf16[8,192,512]{2,1,0:T(8,128)(2,1)}), bf16[8,192,512]{2,1,0:T(8,128)(2,1)S(1)}, u32[]{:S(2)}, u32[]{:S(2)}) %all-to-all-start.3) | async-done | bytes 1572896 | tf_op jit(solution)/shard_map/all_to_all | solution.py:194
  117.4 0.0 copy-done.1
  117.4 0.0 copy-start.2
  117.4 0.8 copy-done.2
  118.2 5.7 %attend.1 = bf16[48,4,2048]{2,1,0:T(4,128)(2,1)} custom-call(bf16[8,192,512]{2,1,0:T(8,128)(2,1)S(1)} %all-to-all-done.3.part_ref, bf16[48,4,2048]{2,1,0:T(4,128)(2,1)S(1)} %copy-done.1, bf16[1152,256]{1,0:T(8,128)(2,1)S(1)} %bitcast.12, bf16[1152,256]{1,0:T(8,128)(2,1)S(1)} %bitcast.13, f32[12,112]{1,0:T(8,128)S(1)} %concatenate.3.clone.mask_ref, ...), custom_call_target="tpu_custom_call" | custom-call | tf_op jit(solution)/shard_map/attend/pallas_call | solution.py:160
  (2 shorter events, 0.0 us)
Async XLA Ops:
  0.6 12.8 %copy-start = (bf16[48,4,2048]{2,1,0:T(4,128)(2,1)S(1)}, bf16[48,4,2048]{2,1,0:T(4,128)(2,1)}, u32[]{:S(2)}) copy-start(bf16[48,4,2048]{2,1,0:T(4,128)(2,1)} %x_ref.1) | copy-start | bytes 2359300
  2.6 28.8 %all-to-all-start = ((bf16[8,2,64,256]{3,2,1,0:T(8,128)(2,1)}), bf16[8,2,64,256]{3,2,1,0:T(8,128)(2,1)S(1)}, u32[]{:S(2)}, u32[]{:S(2)}) async-start(bf16[8,2,64,256]{3,2,1,0:T(8,128)(2,1)} %copy.22), calls=%async_computation | async-start | bytes 1048576 | tf_op jit(solution)/shard_map/all_to_all | solution.py:178
  14.7 20.3 %copy-start.4 = (f32[2,64,256]{2,1,0:T(8,128)S(1)}, f32[2,64,256]{2,1,0:T(8,128)}, u32[]{:S(2)}) copy-start(f32[2,64,256]{2,1,0:T(8,128)} %param.9) | copy-start | bytes 393220
  14.7 20.3 %copy-start.5 = (f32[2,64,256]{2,1,0:T(8,128)S(1)}, f32[2,64,256]{2,1,0:T(8,128)}, u32[]{:S(2)}) copy-start(f32[2,64,256]{2,1,0:T(8,128)} %param.10) | copy-start | bytes 393220
  14.7 20.4 %copy-start.6 = (f32[2,64,256]{2,1,0:T(8,128)S(1)}, f32[2,64,256]{2,1,0:T(8,128)}, u32[]{:S(2)}) copy-start(f32[2,64,256]{2,1,0:T(8,128)} %param.11) | copy-start | bytes 393220
  31.4 13.7 %all-to-all-start.1 = ((bf16[8,192,256]{2,1,0:T(8,128)(2,1)}), bf16[8,192,256]{2,1,0:T(8,128)(2,1)S(1)}, u32[]{:S(2)}, u32[]{:S(2)}) async-start(bf16[8,192,256]{2,1,0:T(8,128)(2,1)} %split_features.1), calls=%async_computation.1 | async-start | bytes 1572864 | tf_op jit(solution)/shard_map/all_to_all | solution.py:184
  46.2 32.6 %all-to-all-start.2 = ((bf16[16,2,64,256]{3,2,1,0:T(8,128)(2,1)}), bf16[16,2,64,256]{3,2,1,0:T(8,128)(2,1)S(1)}, u32[]{:S(2)}, u32[]{:S(2)}) async-start(bf16[16,2,64,256]{3,2,1,0:T(8,128)(2,1)} %broadcast_in_dim.8), calls=%async_computation.2 | async-start | bytes 2097152 | tf_op jit(solution)/shard_map/all_to_all | solution.py:190
  53.5 20.0 %collective-permute-start.1 = (bf16[8,192,256]{2,1,0:T(8,128)(2,1)S(1)}, bf16[8,192,256]{2,1,0:T(8,128)(2,1)S(1)}, u32[]{:S(2)}, u32[]{:S(2)}) collective-permute-start(bf16[8,192,256]{2,1,0:T(8,128)(2,1)S(1)} %all-to-all-done.1.xa), channel_id=1, source_target_pairs={{0,2},{2,0},{1,3},{3,1},{4,6},{6,4},{5,7},{7,5},{8,10},{10,8},{9,1... | collective-permute-start | bytes 2359304 | tf_op jit(solution)/shard_map/ppermute | solution.py:171
  58.2 20.6 %collective-permute-start = (bf16[8,192,256]{2,1,0:T(8,128)(2,1)S(1)}, bf16[8,192,256]{2,1,0:T(8,128)(2,1)S(1)}, u32[]{:S(2)}, u32[]{:S(2)}) collective-permute-start(bf16[8,192,256]{2,1,0:T(8,128)(2,1)S(1)} %all-to-all-done.1.xa), channel_id=1, source_target_pairs={{0,1},{1,0},{2,3},{3,2},{4,5},{5,4},{6,7},{7,6},{8,9},{9,8},{10,11... | collective-permute-start | bytes 2359304 | tf_op jit(solution)/shard_map/ppermute | solution.py:171
  73.5 7.2 %collective-permute-start.2 = (bf16[8,192,256]{2,1,0:T(8,128)(2,1)S(1)}, bf16[8,192,256]{2,1,0:T(8,128)(2,1)}, u32[]{:S(2)}, u32[]{:S(2)}) collective-permute-start(bf16[8,192,256]{2,1,0:T(8,128)(2,1)S(1)} %collective-permute-done.1.xc), channel_id=1, source_target_pairs={{0,1},{1,0},{2,3},{3,2},{4,5},{5,4},{6,7},{7,6},{8,9},{9,8},{10,11... | collective-permute-start | bytes 2359304 | tf_op jit(solution)/shard_map/ppermute | solution.py:171
  84.9 12.7 %copy-start.3 = (bf16[48,24,2,256]{3,2,1,0:T(2,128)(2,1)S(1)}, bf16[48,24,2,256]{3,2,1,0:T(2,128)(2,1)}, u32[]{:S(2)}) copy-start(bf16[48,24,2,256]{3,2,1,0:T(2,128)(2,1)} %param.14) | copy-start | bytes 3538948
  84.9 32.5 %all-to-all-start.3 = ((bf16[8,192,512]{2,1,0:T(8,128)(2,1)}), bf16[8,192,512]{2,1,0:T(8,128)(2,1)S(1)}, u32[]{:S(2)}, u32[]{:S(2)}) async-start(bf16[8,192,512]{2,1,0:T(8,128)(2,1)} %project.1), calls=%async_computation.3 | async-start | bytes 3145728 | tf_op jit(solution)/shard_map/all_to_all | solution.py:194
  99.3 0.7 copy-start.7
  99.3 18.0 %copy-start.1 = (bf16[48,4,2048]{2,1,0:T(4,128)(2,1)S(1)}, bf16[48,4,2048]{2,1,0:T(4,128)(2,1)}, u32[]{:S(2)}) copy-start(bf16[48,4,2048]{2,1,0:T(4,128)(2,1)} %q_ref.1) | copy-start | bytes 2359300
  117.4 0.8 copy-start.2

commit v3 on v2

v3 whole, which is shorter than its diff:
```python
import jax
import jax.numpy as jnp
from jax import lax
from jax.experimental import pallas as pl
from jax.experimental.pallas import tpu as pltpu
from jax.sharding import Mesh
from jax.sharding import PartitionSpec as P

HD = 128
ROWS = 48
STEPS = 4
TOK = ROWS * STEPS
CACHE = 24
FEAT = 2048
COLS = 256
PACK = 4
GROUPS = ROWS // PACK
BATCH = 4
AXES = ("yh", "yl", "xl", "zh", "zl", "xh", "c")
SHARD = ("yh", "yl", "xl", "zh", "zl")
REP = ("yh", "yl", "xl")
FSDP = ("zh", "zl")
TP = ("xh", "c")
CUBE = ("yl", "xl", "zl")
FAR = ("yh", "zh")

beta_one = 0.9
beta_two = 0.95
learning_rate = 0.001
weight_decay = 0.1
epsilon = 1e-08
first_bias = 1.0 - 0.9**10
second_bias = 1.0 - 0.95**10


VM = pl.BlockSpec(memory_space=pltpu.VMEM)
SM = pl.BlockSpec(memory_space=pltpu.SMEM)
PARAMS = pltpu.CompilerParams(vmem_limit_bytes=40 << 20)


def by_owner_kernel(g_ref, o_ref, sems):
    copies = [
        pltpu.make_async_copy(g_ref.at[0, kv], o_ref.at[:, kv], sems.at[kv]) for kv in range(2)
    ]
    for copy in copies:
        copy.start()
    for copy in copies:
        copy.wait()


def by_owner(grads):
    return pl.pallas_call(
        by_owner_kernel,
        out_shape=jax.ShapeDtypeStruct((8, 2, 64, COLS), jnp.bfloat16),
        in_specs=[pl.BlockSpec(memory_space=pltpu.HBM)],
        out_specs=VM,
        scratch_shapes=[pltpu.SemaphoreType.DMA((2,))],
        compiler_params=pltpu.CompilerParams(vmem_limit_bytes=60 << 20),
        name="by_owner",
    )(grads)


def adamw_kernel(g_ref, w_ref, one_ref, two_ref, new_w_ref, new_one_ref, new_two_ref, copies_ref):
    gradient = g_ref[0].astype(jnp.float32)
    for j in range(1, 8):
        gradient = gradient + g_ref[j].astype(jnp.float32)
    master = w_ref[...]
    new_one = beta_one * one_ref[...] + (1.0 - beta_one) * gradient
    new_two = beta_two * two_ref[...] + (1.0 - beta_two) * gradient * gradient
    update = new_one / first_bias / (jnp.sqrt(new_two / second_bias) + epsilon)
    new_master = master - learning_rate * (update + weight_decay * master)
    new_one_ref[...] = new_one
    new_two_ref[...] = new_two
    new_w_ref[...] = new_master
    rollout = new_master.astype(jnp.bfloat16)
    for j in range(16):
        copies_ref[j] = rollout


def adamw(pieces, master, moment_one, moment_two):
    kept = jax.ShapeDtypeStruct(master.shape, jnp.float32)
    return pl.pallas_call(
        adamw_kernel,
        out_shape=(kept, kept, kept, jax.ShapeDtypeStruct((16,) + master.shape, jnp.bfloat16)),
        in_specs=[VM] * 4,
        out_specs=(VM,) * 4,
        compiler_params=PARAMS,
        name="adamw",
    )(pieces, master, moment_one, moment_two)


def split_kernel(me_ref, x_ref, *refs):
    blocks = refs[4]
    for b in range(4):
        v = [
            x_ref[:, :, 512 * b + 128 * k : 512 * b + 128 * (k + 1)].reshape(TOK, 128)
            for k in range(4)
        ]
        for half in range(2):
            cut = slice(64 * half, 64 * (half + 1))
            for p in range(2):
                blocks[2 * b + half, :, 128 * p : 128 * (p + 1)] = jnp.concatenate(
                    [v[2 * p][:, cut], v[2 * p + 1][:, cut]], axis=1
                )
    for p in range(4):
        for d in range(2):
            refs[p][d] = blocks[me_ref[0] ^ (2 * p + d)]


def split_features(me, x):
    pair = jax.ShapeDtypeStruct((2, TOK, COLS), jnp.bfloat16)
    return pl.pallas_call(
        split_kernel,
        out_shape=(pair,) * 4,
        in_specs=[SM, VM],
        out_specs=(VM,) * 4,
        scratch_shapes=[pltpu.VMEM((8, TOK, COLS), jnp.bfloat16)],
        compiler_params=PARAMS,
        name="split_features",
    )(me, x)


def project_kernel(me_ref, t_ref, xa, xb, xc, xd, w_ref, o_ref):
    me, own = me_ref[0], t_ref[0]
    for kv in range(2):
        w = jnp.concatenate(
            [w_ref[pl.ds(4 * (own ^ f), 4), kv].reshape(COLS, COLS) for f in range(4)], axis=0
        )
        for m in range(0, 8, 2):
            x = jnp.concatenate(
                [r[m : m + 2].reshape(2 * TOK, COLS) for r in (xa, xb, xc, xd)], axis=1
            )
            y = jnp.dot(x, w, preferred_element_type=jnp.float32).astype(jnp.bfloat16)
            for d in range(m, m + 2):
                o_ref[me ^ (2 * (d % 4) + d // 4), :, kv * COLS : (kv + 1) * COLS] = y[
                    TOK * (d - m) : TOK * (d - m + 1)
                ]


def project(me, own, features, w):
    return pl.pallas_call(
        project_kernel,
        out_shape=jax.ShapeDtypeStruct((8, TOK, 2 * COLS), jnp.bfloat16),
        in_specs=[SM] * 2 + [VM] * 5,
        out_specs=VM,
        compiler_params=PARAMS,
        name="project",
    )(me, own, *features, w)


def seen_bias(axis):
    width, old, count = PACK * (CACHE + STEPS), PACK * CACHE, 8 * PACK * STEPS
    shape = (count, width) if axis == 1 else (width, count)
    row = lax.broadcasted_iota(jnp.int32, shape, 1 - axis)
    col = lax.broadcasted_iota(jnp.int32, shape, axis)
    own = (row // STEPS) % PACK
    of_col = jnp.where(col < old, col // CACHE, (col - old) // STEPS)
    seen = (own == of_col) & ((col < old) | ((col - old) % STEPS <= row % STEPS))
    return jnp.where(seen, 0.0, -jnp.inf)


def length_bias(axis, lens):
    old = PACK * CACHE
    width = old + PACK * STEPS
    col = lax.broadcasted_iota(jnp.int32, (8, width) if axis == 1 else (width, 8 * PACK * STEPS), axis)
    limit = jnp.where(col < old, -1, width)
    for r in range(PACK):
        limit = jnp.where(col // CACHE == r, CACHE * r + lens[r], limit)
    return jnp.where(col < limit, 0.0, -jnp.inf)


def attend_kernel(lens_ref, part_ref, q_ref, k_ref, v_ref, o_ref):
    old, new = PACK * CACHE, PACK * STEPS
    width, count = old + new, 8 * new
    scale = 1.4426950408889634 / HD**0.5
    base, base_t = seen_bias(1), seen_bias(0)
    eye = lax.broadcasted_iota(jnp.int32, (count, count), 0) == lax.broadcasted_iota(
        jnp.int32, (count, count), 1
    )
    minus = jnp.full((width, count), -1.0, jnp.bfloat16)
    ones = jnp.ones((width, HD), jnp.bfloat16)
    heads = [[slice(HD * (8 * g + h), HD * (8 * g + h + 1)) for h in range(8)] for g in range(2)]
    across = (((1,), (1,)), ((), ()))
    for first in range(0, GROUPS, BATCH):
        units = []
        for i in range(first, first + BATCH):
            fresh = part_ref[0, new * i : new * (i + 1), :].astype(jnp.float32)
            for j in range(1, 8):
                fresh = fresh + part_ref[j, new * i : new * (i + 1), :].astype(jnp.float32)
            fresh = fresh.astype(jnp.bfloat16)
            rows = slice(PACK * i, PACK * (i + 1))
            past = slice(old * i, old * (i + 1))
            lens = [lens_ref[PACK * i + r] for r in range(PACK)]
            for g in range(2):
                k_lanes = slice(HD * g, HD * (g + 1))
                v_lanes = slice(COLS + HD * g, COLS + HD * (g + 1))
                q = jnp.concatenate([q_ref[rows, :, h].reshape(new, HD) for h in heads[g]], axis=0)
                k = jnp.concatenate([k_ref[past, k_lanes], fresh[:, k_lanes]], axis=0)
                v = jnp.concatenate([v_ref[past, k_lanes], fresh[:, v_lanes]], axis=0)
                units.append((rows, g, lens, q, k, v))
        turned = [
            lax.dot_general(k, q, across, preferred_element_type=jnp.float32)
            for rows, g, lens, q, k, v in units
        ]
        shifts = []
        for t, (rows, g, lens, q, k, v) in zip(turned, units):
            top = jnp.max(t + (base_t + length_bias(0, lens)), axis=0, keepdims=True)
            shifts.append(jnp.where(eye, top, 0.0).astype(jnp.bfloat16))
        scores = [
            lax.dot_general(
                jnp.concatenate([q, shift], axis=1),
                jnp.concatenate([k, minus], axis=1),
                across,
                preferred_element_type=jnp.float32,
            )
            for shift, (rows, g, lens, q, k, v) in zip(shifts, units)
        ]
        weights = [
            jnp.exp2(s * scale + (base + length_bias(1, lens)[0:1])).astype(jnp.bfloat16)
            for s, (rows, g, lens, q, k, v) in zip(scores, units)
        ]
        outs = [
            jnp.dot(e, jnp.concatenate([v, ones], axis=1), preferred_element_type=jnp.float32)
            for e, (rows, g, lens, q, k, v) in zip(weights, units)
        ]
        for out, (rows, g, lens, q, k, v) in zip(outs, units):
            out = (out[:, :HD] / out[:, HD:]).astype(jnp.bfloat16)
            for n, h in enumerate(heads[g]):
                o_ref[rows, :, h] = out[new * n : new * (n + 1)].reshape(PACK, STEPS, HD)


def attend(lengths, parts, q, keys, values):
    return pl.pallas_call(
        attend_kernel,
        out_shape=jax.ShapeDtypeStruct((ROWS, STEPS, FEAT), jnp.bfloat16),
        in_specs=[SM] + [VM] * 4,
        out_specs=VM,
        compiler_params=PARAMS,
        name="attend",
    )(lengths, parts, q, keys, values)


def flipped(x, axis):
    return lax.ppermute(x, axis, [(0, 1), (1, 0)])


def on_device(
    grad_parts, master_weight, moment_one, moment_two, layer_inputs, queries, kv_cache, lengths
):
    me = lax.axis_index(CUBE).astype(jnp.int32).reshape(1)
    own = lax.axis_index(TP).astype(jnp.int32).reshape(1)

    pieces = by_owner(grad_parts.reshape(1, 2, 8, 64, COLS))
    pieces = lax.all_to_all(pieces, FSDP, 0, 0, tiled=True)
    new_master, new_one, new_two, copies = adamw(pieces, master_weight, moment_one, moment_two)

    pairs = split_features(me, layer_inputs)
    pairs = [pairs[0]] + [
        lax.ppermute(pairs[p], ("yl", "xl"), [(i, i ^ p) for i in range(4)]) for p in range(1, 4)
    ]
    far = flipped(jnp.concatenate([pair[1:2] for pair in pairs]), "zl")
    features = jnp.concatenate([pair[0:1] for pair in pairs] + [far])
    beside = flipped(features, "c")
    across = flipped(features, "xh")
    beyond = flipped(across, "c")

    weight = lax.all_to_all(copies, FAR, 0, 0, tiled=True)

    partial = project(me, own, (features, beside, across, beyond), weight)
    partial = lax.all_to_all(partial, CUBE, 0, 0, tiled=True)

    keys = kv_cache[:, :, 0].reshape(ROWS * CACHE, COLS)
    values = kv_cache[:, :, 1].reshape(ROWS * CACHE, COLS)
    context = attend(lengths, partial, queries, keys, values)
    return (new_master, new_one, new_two, context)


def solution(mesh):
    finer = Mesh(mesh.devices.reshape(4, 2, 2, 4, 2, 2, 2), AXES)
    shard = P(None, SHARD, TP)
    return jax.shard_map(
        on_device,
        mesh=finer,
        in_specs=(
            P(FSDP, None, REP, TP),
            shard,
            shard,
            shard,
            P(SHARD, None, TP),
            P(SHARD, None, TP),
            P(SHARD, None, None, TP),
            P(SHARD),
        ),
        out_specs=(shard, shard, shard, P(SHARD, None, TP)),
        check_vma=False,
    )
```

time: 125 us -> 110 us (0.88)
  waiting for transfers between devices: 52.8 us -> 40.2 us
  local copies, waits for them, and re-layouts: 8.84 us -> 1.95 us
  starting transfers between devices: 48.8 us -> 55.6 us
  other arithmetic: 1.57 us -> 0.05 us
    all_to_all x1, waiting for transfers between devices: 16.7 us -> 0.05 us  [on_device(): pieces = lax.all_to_all(pieces, FSDP, 0, 0, tiled=True)]
    ppermute x0 -> x3, starting transfers between devices: none -> 8.37 us  [on_device(): lax.ppermute(pairs[p], ('yl', 'xl'), [(i, i ^ p) for i in range(4)])]
    all_to_all x2 -> x1, waiting for transfers between devices: 9.2 us -> 3.38 us  [on_device(): weight = lax.all_to_all(copies, FAR, 0, 0, tiled=True)]
    ppermute x0 -> x3, waiting for transfers between devices: none -> 5.65 us  [on_device(): lax.ppermute(pairs[p], ('yl', 'xl'), [(i, i ^ p) for i in range(4)])]
    all_to_all x1, starting transfers between devices: 12.7 us -> 7.29 us  [on_device(): partial = lax.all_to_all(partial, CUBE, 0, 0, tiled=True)]
    all_to_all x1, waiting for transfers between devices: 14.1 us -> 18.2 us  [on_device(): partial = lax.all_to_all(partial, CUBE, 0, 0, tiled=True)]
    transpose x2 -> x0, local copies, waits for them, and re-layouts: 3.4 us -> none  [the longest x1 1.97 us: on_device(): pieces = jnp.moveaxis(grad_parts[0].reshape(2, 8, 64, COLS), 1, 0)]
    ppermute x3 -> x4, starting transfers between devices: 14.4 us -> 17.5 us  [flipped(): return lax.ppermute(x, axis, [(0, 1), (1, 0)])]
  transfers between devices with their start and end apart: 7 -> 10, of which waited for: 5 -> 6; matrix products, arithmetic and copies ran while one was open for 5% -> 2% of each run, Pallas kernels for 1% -> 2%
where the time goes in v3:
time: 110 us
  starting transfers between devices  55.6 us (51%)
  waiting for transfers between devices  40.2 us (37%)
  Pallas kernels  10.8 us (10%)
  local copies, waits for them, and re-layouts  1.95 us (2%)
    all_to_all x1, waiting for transfers between devices, on_device(): partial = lax.all_to_all(partial, CUBE, 0, 0, tiled=True)  18.2 us
    ppermute x4, starting transfers between devices, flipped(): return lax.ppermute(x, axis, [(0, 1), (1, 0)])  17.5 us
    ppermute x4, waiting for transfers between devices, flipped(): return lax.ppermute(x, axis, [(0, 1), (1, 0)])  13 us
    all_to_all x1, starting transfers between devices, on_device(): weight = lax.all_to_all(copies, FAR, 0, 0, tiled=True)  11.6 us
    all_to_all x1, starting transfers between devices, on_device(): pieces = lax.all_to_all(pieces, FSDP, 0, 0, tiled=True)  10.9 us
    ppermute x3, starting transfers between devices, on_device(): lax.ppermute(pairs[p], ('yl', 'xl'), [(i, i ^ p) for i in range(4)])  8.37 us
    all_to_all x1, starting transfers between devices, on_device(): partial = lax.all_to_all(partial, CUBE, 0, 0, tiled=True)  7.29 us
    ppermute x3, waiting for transfers between devices, on_device(): lax.ppermute(pairs[p], ('yl', 'xl'), [(i, i ^ p) for i in range(4)])  5.65 us
  transfers between devices with their start and end apart: 10, of which 6 were waited for; matrix products, arithmetic and copies ran while one was open for 2% of the time, Pallas kernels for 2%

profile of v3, /device:TPU:1, one launch (start us, length us, event | category | flops | bytes accessed | tf_op | source)
XLA Modules:
  0.0 109.6 jit_solution(11795523335457930383)
XLA Ops:
  0.6 0.0 copy-start.1
  0.6 1.9 %by_owner.1 = bf16[8,2,64,256]{3,2,1,0:T(8,128)(2,1)} custom-call(bf16[1,2,8,64,256]{4,3,2,1,0:T(8,128)(2,1)} %bitcast.7), custom_call_target="tpu_custom_call" | custom-call | tf_op jit(solution)/shard_map/by_owner/pallas_call | solution.py:52
  2.6 10.9 %all-to-all-start = ((bf16[8,2,64,256]{3,2,1,0:T(8,128)(2,1)}), bf16[8,2,64,256]{3,2,1,0:T(8,128)(2,1)S(1)}, u32[]{:S(2)}, u32[]{:S(2)}) async-start(bf16[8,2,64,256]{3,2,1,0:T(8,128)(2,1)} %by_owner.1), calls=%async_computation | async-start | bytes 1048576 | tf_op jit(solution)/shard_map/all_to_all | solution.py:254
  13.4 0.0 copy-done.1
  13.4 0.4 split_features.1
  13.9 3.1 %collective-permute-start = (bf16[2,192,256]{2,1,0:T(8,128)(2,1)S(1)}, bf16[2,192,256]{2,1,0:T(8,128)(2,1)S(1)}, u32[]{:S(2)}, u32[]{:S(2)}) collective-permute-start(bf16[2,192,256]{2,1,0:T(8,128)(2,1)S(1)} %get-tuple-element.16), channel_id=1, source_target_pairs={{0,32},{32,0},{64,96},{96,64},{1,33},{33,1},{65,97},{97,65},{2,34}... | collective-permute-start | bytes 589832 | tf_op jit(solution)/shard_map/ppermute | solution.py:259
  17.0 3.2 %collective-permute-start.1 = (bf16[2,192,256]{2,1,0:T(8,128)(2,1)S(1)}, bf16[2,192,256]{2,1,0:T(8,128)(2,1)S(1)}, u32[]{:S(2)}, u32[]{:S(2)}) collective-permute-start(bf16[2,192,256]{2,1,0:T(8,128)(2,1)S(1)} %get-tuple-element.17), channel_id=1, source_target_pairs={{0,64},{32,96},{64,0},{96,32},{1,65},{33,97},{65,1},{97,33},{2,66}... | collective-permute-start | bytes 589832 | tf_op jit(solution)/shard_map/ppermute | solution.py:259
  20.2 2.0 %collective-permute-start.2 = (bf16[2,192,256]{2,1,0:T(8,128)(2,1)S(1)}, bf16[2,192,256]{2,1,0:T(8,128)(2,1)S(1)}, u32[]{:S(2)}, u32[]{:S(2)}) collective-permute-start(bf16[2,192,256]{2,1,0:T(8,128)(2,1)S(1)} %get-tuple-element.18), channel_id=1, source_target_pairs={{0,96},{32,64},{64,32},{96,0},{1,97},{33,65},{65,33},{97,1},{2,98}... | collective-permute-start | bytes 589832 | tf_op jit(solution)/shard_map/ppermute | solution.py:259
  22.3 0.0 copy-start.2
  22.3 0.0 copy-start.3
  22.3 0.0 copy-start.4
  22.3 0.0 collective-permute-done
  22.4 1.7 %collective-permute-done.1 = bf16[2,192,256]{2,1,0:T(8,128)(2,1)S(1)} collective-permute-done((bf16[2,192,256]{2,1,0:T(8,128)(2,1)S(1)}, bf16[2,192,256]{2,1,0:T(8,128)(2,1)S(1)}, u32[]{:S(2)}, u32[]{:S(2)}) %collective-permute-start.1) | collective-permute-done | bytes 196640 | tf_op jit(solution)/shard_map/ppermute | solution.py:259
  24.1 4.0 %collective-permute-done.2 = bf16[2,192,256]{2,1,0:T(8,128)(2,1)S(1)} collective-permute-done((bf16[2,192,256]{2,1,0:T(8,128)(2,1)S(1)}, bf16[2,192,256]{2,1,0:T(8,128)(2,1)S(1)}, u32[]{:S(2)}, u32[]{:S(2)}) %collective-permute-start.2) | collective-permute-done | bytes 196640 | tf_op jit(solution)/shard_map/ppermute | solution.py:259
  28.1 0.1 pad_maximum_fusion
  28.1 3.2 %collective-permute-start.3 = (bf16[4,192,256]{2,1,0:T(8,128)(2,1)S(1)}, bf16[4,192,256]{2,1,0:T(8,128)(2,1)S(1)}, u32[]{:S(2)}, u32[]{:S(2)}) collective-permute-start(bf16[4,192,256]{2,1,0:T(8,128)(2,1)S(1)} %pad_maximum_fusion), channel_id=1, source_target_pairs={{0,4},{4,0},{1,5},{5,1},{2,6},{6,2},{3,7},{7,3},{8,12},{12,8},{9,1... | collective-permute-start | bytes 1179656 | tf_op jit(solution)/shard_map/ppermute | solution.py:244
  31.3 0.0 all-to-all-done.g_ref
  31.4 0.0 copy-done.2
  31.4 0.0 copy-done.3
  31.4 0.0 copy-done.4
  31.4 1.3 %adamw.1 = (f32[2,64,256]{2,1,0:T(8,128)}, f32[2,64,256]{2,1,0:T(8,128)}, f32[2,64,256]{2,1,0:T(8,128)}, bf16[16,2,64,256]{3,2,1,0:T(8,128)(2,1)}) custom-call(bf16[8,2,64,256]{3,2,1,0:T(8,128)(2,1)S(1)} %all-to-all-done.g_ref, f32[2,64,256]{2,1,0:T(8,128)S(1)} %copy-done.2, f32[2,64,256]{2,1,0:T(8,128)S(1)} %copy-done.3, f32[2,64,256]{2,1,0:T(8,128)S(1)} %copy-done.4), custom_call_target="tpu_custom_call" | custom-call | tf_op jit(solution)/shard_map/adamw/pallas_call | solution.py:82
  32.7 11.6 %all-to-all-start.1 = ((bf16[16,2,64,256]{3,2,1,0:T(8,128)(2,1)}), bf16[16,2,64,256]{3,2,1,0:T(8,128)(2,1)S(1)}, u32[]{:S(2)}, u32[]{:S(2)}) async-start(bf16[16,2,64,256]{3,2,1,0:T(8,128)(2,1)} %get-tuple-element.19), calls=%async_computation.1 | async-start | bytes 2097152 | tf_op jit(solution)/shard_map/all_to_all | solution.py:267
  44.3 0.0 collective-permute-done.3
  44.4 4.7 %collective-permute-start.5 = (bf16[8,192,256]{2,1,0:T(8,128)(2,1)S(1)}, bf16[8,192,256]{2,1,0:T(8,128)(2,1)S(1)}, u32[]{:S(2)}, u32[]{:S(2)}) collective-permute-start(bf16[8,192,256]{2,1,0:T(8,128)(2,1)S(1)} %constant_dynamic-update-slice_fusion.xa), channel_id=1, source_target_pairs={{0,2},{2,0},{1,3},{3,1},{4,6},{6,4},{5,7},{7,5},{8,10},{10,8},{9,1... | collective-permute-start | bytes 2359304 | tf_op jit(solution)/shard_map/ppermute | solution.py:244
  49.1 4.4 %collective-permute-start.4 = (bf16[8,192,256]{2,1,0:T(8,128)(2,1)S(1)}, bf16[8,192,256]{2,1,0:T(8,128)(2,1)S(1)}, u32[]{:S(2)}, u32[]{:S(2)}) collective-permute-start(bf16[8,192,256]{2,1,0:T(8,128)(2,1)S(1)} %constant_dynamic-update-slice_fusion.xa), channel_id=1, source_target_pairs={{0,1},{1,0},{2,3},{3,2},{4,5},{5,4},{6,7},{7,6},{8,9},{9,8},{10,11... | collective-permute-start | bytes 2359304 | tf_op jit(solution)/shard_map/ppermute | solution.py:244
  53.5 11.0 %collective-permute-done.5.xc = bf16[8,192,256]{2,1,0:T(8,128)(2,1)S(1)} collective-permute-done((bf16[8,192,256]{2,1,0:T(8,128)(2,1)S(1)}, bf16[8,192,256]{2,1,0:T(8,128)(2,1)S(1)}, u32[]{:S(2)}, u32[]{:S(2)}) %collective-permute-start.5) | collective-permute-done | bytes 786464 | tf_op jit(solution)/shard_map/ppermute | solution.py:244
  64.5 5.1 %collective-permute-start.6 = (bf16[8,192,256]{2,1,0:T(8,128)(2,1)S(1)}, bf16[8,192,256]{2,1,0:T(8,128)(2,1)}, u32[]{:S(2)}, u32[]{:S(2)}) collective-permute-start(bf16[8,192,256]{2,1,0:T(8,128)(2,1)S(1)} %collective-permute-done.5.xc), channel_id=1, source_target_pairs={{0,1},{1,0},{2,3},{3,2},{4,5},{5,4},{6,7},{7,6},{8,9},{9,8},{10,11... | collective-permute-start | bytes 2359304 | tf_op jit(solution)/shard_map/ppermute | solution.py:244
  69.6 0.0 collective-permute-done.4.xb
  69.6 2.0 %collective-permute-done.6.xd = bf16[8,192,256]{2,1,0:T(8,128)(2,1)} collective-permute-done((bf16[8,192,256]{2,1,0:T(8,128)(2,1)S(1)}, bf16[8,192,256]{2,1,0:T(8,128)(2,1)}, u32[]{:S(2)}, u32[]{:S(2)}) %collective-permute-start.6) | collective-permute-done | bytes 786464 | tf_op jit(solution)/shard_map/ppermute | solution.py:244
  71.6 3.4 %all-to-all-done.1.w_ref = bf16[16,2,64,256]{3,2,1,0:T(8,128)(2,1)S(1)} async-done(((bf16[16,2,64,256]{3,2,1,0:T(8,128)(2,1)}), bf16[16,2,64,256]{3,2,1,0:T(8,128)(2,1)S(1)}, u32[]{:S(2)}, u32[]{:S(2)}) %all-to-all-start.1) | async-done | bytes 1048608 | tf_op jit(solution)/shard_map/all_to_all | solution.py:267
  75.0 4.2 %project.1 = bf16[8,192,512]{2,1,0:T(8,128)(2,1)} custom-call(s32[1]{0:T(128)} %bitcast.1.me_ref, s32[1]{0:T(128)} %bitcast.2.t_ref, bf16[8,192,256]{2,1,0:T(8,128)(2,1)S(1)} %constant_dynamic-update-slice_fusion.xa, bf16[8,192,256]{2,1,0:T(8,128)(2,1)S(1)} %collective-permute-done.4.xb, bf16[8,192,256]{2,1,0:T(8,128)(2,1)S(1)} %collective-permute-done.5.xc, ...), custom_call_target="tpu_custom_call" | custom-call | tf_op jit(solution)/shard_map/project/pallas_call | solution.py:141
  79.2 0.0 copy-start.6
  79.2 7.3 %all-to-all-start.2 = ((bf16[8,192,512]{2,1,0:T(8,128)(2,1)}), bf16[8,192,512]{2,1,0:T(8,128)(2,1)S(1)}, u32[]{:S(2)}, u32[]{:S(2)}) async-start(bf16[8,192,512]{2,1,0:T(8,128)(2,1)} %project.1), calls=%async_computation.2 | async-start | bytes 3145728 | tf_op jit(solution)/shard_map/all_to_all | solution.py:270
  86.5 0.0 copy-done.6
  86.5 1.6 %fusion = (bf16[48,24,1,256]{3,2,1,0:T(2,128)(2,1)S(1)}, bf16[48,24,1,256]{3,2,1,0:T(2,128)(2,1)S(1)}) fusion(bf16[48,24,2,256]{3,2,1,0:T(2,128)(2,1)S(1)} %copy-done.6), kind=kLoop, calls=%fused_computation.6 | loop fusion | bytes 2359296 | tf_op jit(solution)/shard_map/slice | solution.py:273
  88.1 0.1 copy.15
  88.2 0.0 copy-start
  88.2 0.0 copy-start.5
  88.3 0.1 copy.14
  88.4 18.2 %all-to-all-done.2.part_ref = bf16[8,192,512]{2,1,0:T(8,128)(2,1)S(1)} async-done(((bf16[8,192,512]{2,1,0:T(8,128)(2,1)}), bf16[8,192,512]{2,1,0:T(8,128)(2,1)S(1)}, u32[]{:S(2)}, u32[]{:S(2)}) %all-to-all-start.2) | async-done | bytes 1572896 | tf_op jit(solution)/shard_map/all_to_all | solution.py:270
  106.5 0.0 copy-done
  106.5 0.0 copy-done.5
  106.5 3.0 %attend.1 = bf16[48,4,2048]{2,1,0:T(4,128)(2,1)} custom-call(s32[48]{0:T(128)S(1)} %copy-done.5, bf16[8,192,512]{2,1,0:T(8,128)(2,1)S(1)} %all-to-all-done.2.part_ref, bf16[48,4,2048]{2,1,0:T(4,128)(2,1)S(1)} %copy-done, bf16[1152,256]{1,0:T(8,128)(2,1)S(1)} %bitcast.6, bf16[1152,256]{1,0:T(8,128)(2,1)S(1)} %bitcast.5), custom_call_target="tpu_custom_call" | custom-call | tf_op jit(solution)/shard_map/attend/pallas_call | solution.py:233
  (5 shorter events, 0.1 us)
Async XLA Ops:
  0.6 12.8 %copy-start.1 = (bf16[48,4,2048]{2,1,0:T(4,128)(2,1)S(1)}, bf16[48,4,2048]{2,1,0:T(4,128)(2,1)}, u32[]{:S(2)}) copy-start(bf16[48,4,2048]{2,1,0:T(4,128)(2,1)} %x_ref.1) | copy-start | bytes 2359300
  2.6 28.8 %all-to-all-start = ((bf16[8,2,64,256]{3,2,1,0:T(8,128)(2,1)}), bf16[8,2,64,256]{3,2,1,0:T(8,128)(2,1)S(1)}, u32[]{:S(2)}, u32[]{:S(2)}) async-start(bf16[8,2,64,256]{3,2,1,0:T(8,128)(2,1)} %by_owner.1), calls=%async_computation | async-start | bytes 1048576 | tf_op jit(solution)/shard_map/all_to_all | solution.py:254
  13.9 8.5 %collective-permute-start = (bf16[2,192,256]{2,1,0:T(8,128)(2,1)S(1)}, bf16[2,192,256]{2,1,0:T(8,128)(2,1)S(1)}, u32[]{:S(2)}, u32[]{:S(2)}) collective-permute-start(bf16[2,192,256]{2,1,0:T(8,128)(2,1)S(1)} %get-tuple-element.16), channel_id=1, source_target_pairs={{0,32},{32,0},{64,96},{96,64},{1,33},{33,1},{65,97},{97,65},{2,34}... | collective-permute-start | bytes 589832 | tf_op jit(solution)/shard_map/ppermute | solution.py:259
  17.0 7.0 %collective-permute-start.1 = (bf16[2,192,256]{2,1,0:T(8,128)(2,1)S(1)}, bf16[2,192,256]{2,1,0:T(8,128)(2,1)S(1)}, u32[]{:S(2)}, u32[]{:S(2)}) collective-permute-start(bf16[2,192,256]{2,1,0:T(8,128)(2,1)S(1)} %get-tuple-element.17), channel_id=1, source_target_pairs={{0,64},{32,96},{64,0},{96,32},{1,65},{33,97},{65,1},{97,33},{2,66}... | collective-permute-start | bytes 589832 | tf_op jit(solution)/shard_map/ppermute | solution.py:259
  20.2 7.8 %collective-permute-start.2 = (bf16[2,192,256]{2,1,0:T(8,128)(2,1)S(1)}, bf16[2,192,256]{2,1,0:T(8,128)(2,1)S(1)}, u32[]{:S(2)}, u32[]{:S(2)}) collective-permute-start(bf16[2,192,256]{2,1,0:T(8,128)(2,1)S(1)} %get-tuple-element.18), channel_id=1, source_target_pairs={{0,96},{32,64},{64,32},{96,0},{1,97},{33,65},{65,33},{97,1},{2,98}... | collective-permute-start | bytes 589832 | tf_op jit(solution)/shard_map/ppermute | solution.py:259
  22.3 9.1 %copy-start.2 = (f32[2,64,256]{2,1,0:T(8,128)S(1)}, f32[2,64,256]{2,1,0:T(8,128)}, u32[]{:S(2)}) copy-start(f32[2,64,256]{2,1,0:T(8,128)} %w_ref.1) | copy-start | bytes 393220
  22.3 9.1 %copy-start.3 = (f32[2,64,256]{2,1,0:T(8,128)S(1)}, f32[2,64,256]{2,1,0:T(8,128)}, u32[]{:S(2)}) copy-start(f32[2,64,256]{2,1,0:T(8,128)} %one_ref.1) | copy-start | bytes 393220
  22.3 9.1 %copy-start.4 = (f32[2,64,256]{2,1,0:T(8,128)S(1)}, f32[2,64,256]{2,1,0:T(8,128)}, u32[]{:S(2)}) copy-start(f32[2,64,256]{2,1,0:T(8,128)} %two_ref.1) | copy-start | bytes 393220
  28.1 16.2 %collective-permute-start.3 = (bf16[4,192,256]{2,1,0:T(8,128)(2,1)S(1)}, bf16[4,192,256]{2,1,0:T(8,128)(2,1)S(1)}, u32[]{:S(2)}, u32[]{:S(2)}) collective-permute-start(bf16[4,192,256]{2,1,0:T(8,128)(2,1)S(1)} %pad_maximum_fusion), channel_id=1, source_target_pairs={{0,4},{4,0},{1,5},{5,1},{2,6},{6,2},{3,7},{7,3},{8,12},{12,8},{9,1... | collective-permute-start | bytes 1179656 | tf_op jit(solution)/shard_map/ppermute | solution.py:244
  32.7 42.3 %all-to-all-start.1 = ((bf16[16,2,64,256]{3,2,1,0:T(8,128)(2,1)}), bf16[16,2,64,256]{3,2,1,0:T(8,128)(2,1)S(1)}, u32[]{:S(2)}, u32[]{:S(2)}) async-start(bf16[16,2,64,256]{3,2,1,0:T(8,128)(2,1)} %get-tuple-element.19), calls=%async_computation.1 | async-start | bytes 2097152 | tf_op jit(solution)/shard_map/all_to_all | solution.py:267
  44.4 20.1 %collective-permute-start.5 = (bf16[8,192,256]{2,1,0:T(8,128)(2,1)S(1)}, bf16[8,192,256]{2,1,0:T(8,128)(2,1)S(1)}, u32[]{:S(2)}, u32[]{:S(2)}) collective-permute-start(bf16[8,192,256]{2,1,0:T(8,128)(2,1)S(1)} %constant_dynamic-update-slice_fusion.xa), channel_id=1, source_target_pairs={{0,2},{2,0},{1,3},{3,1},{4,6},{6,4},{5,7},{7,5},{8,10},{10,8},{9,1... | collective-permute-start | bytes 2359304 | tf_op jit(solution)/shard_map/ppermute | solution.py:244
  49.1 20.5 %collective-permute-start.4 = (bf16[8,192,256]{2,1,0:T(8,128)(2,1)S(1)}, bf16[8,192,256]{2,1,0:T(8,128)(2,1)S(1)}, u32[]{:S(2)}, u32[]{:S(2)}) collective-permute-start(bf16[8,192,256]{2,1,0:T(8,128)(2,1)S(1)} %constant_dynamic-update-slice_fusion.xa), channel_id=1, source_target_pairs={{0,1},{1,0},{2,3},{3,2},{4,5},{5,4},{6,7},{7,6},{8,9},{9,8},{10,11... | collective-permute-start | bytes 2359304 | tf_op jit(solution)/shard_map/ppermute | solution.py:244
  64.5 7.2 %collective-permute-start.6 = (bf16[8,192,256]{2,1,0:T(8,128)(2,1)S(1)}, bf16[8,192,256]{2,1,0:T(8,128)(2,1)}, u32[]{:S(2)}, u32[]{:S(2)}) collective-permute-start(bf16[8,192,256]{2,1,0:T(8,128)(2,1)S(1)} %collective-permute-done.5.xc), channel_id=1, source_target_pairs={{0,1},{1,0},{2,3},{3,2},{4,5},{5,4},{6,7},{7,6},{8,9},{9,8},{10,11... | collective-permute-start | bytes 2359304 | tf_op jit(solution)/shard_map/ppermute | solution.py:244
  79.2 7.3 %copy-start.6 = (bf16[48,24,2,256]{3,2,1,0:T(2,128)(2,1)S(1)}, bf16[48,24,2,256]{3,2,1,0:T(2,128)(2,1)}, u32[]{:S(2)}) copy-start(bf16[48,24,2,256]{3,2,1,0:T(2,128)(2,1)} %param.14) | copy-start | bytes 3538948
  79.2 27.4 %all-to-all-start.2 = ((bf16[8,192,512]{2,1,0:T(8,128)(2,1)}), bf16[8,192,512]{2,1,0:T(8,128)(2,1)S(1)}, u32[]{:S(2)}, u32[]{:S(2)}) async-start(bf16[8,192,512]{2,1,0:T(8,128)(2,1)} %project.1), calls=%async_computation.2 | async-start | bytes 3145728 | tf_op jit(solution)/shard_map/all_to_all | solution.py:270
  88.2 18.3 %copy-start = (bf16[48,4,2048]{2,1,0:T(4,128)(2,1)S(1)}, bf16[48,4,2048]{2,1,0:T(4,128)(2,1)}, u32[]{:S(2)}) copy-start(bf16[48,4,2048]{2,1,0:T(4,128)(2,1)} %q_ref.1) | copy-start | bytes 2359300
  88.2 18.3 %copy-start.5 = (s32[48]{0:T(128)S(1)}, s32[48]{0:T(128)}, u32[]{:S(2)}) copy-start(s32[48]{0:T(128)} %lens_ref.1) | copy-start | bytes 580

commit v4 on v3

--- a/solution.py
+++ b/solution.py
@@ -130,7 +130,7 @@
             x = jnp.concatenate(
                 [r[m : m + 2].reshape(2 * TOK, COLS) for r in (xa, xb, xc, xd)], axis=1
             )
-            y = jnp.dot(x, w, preferred_element_type=jnp.float32).astype(jnp.bfloat16)
+            y = jnp.dot(x, w, preferred_element_type=jnp.float32)
             for d in range(m, m + 2):
                 o_ref[me ^ (2 * (d % 4) + d // 4), :, kv * COLS : (kv + 1) * COLS] = y[
                     TOK * (d - m) : TOK * (d - m + 1)
@@ -140,7 +140,7 @@
 def project(me, own, features, w):
     return pl.pallas_call(
         project_kernel,
-        out_shape=jax.ShapeDtypeStruct((8, TOK, 2 * COLS), jnp.bfloat16),
+        out_shape=jax.ShapeDtypeStruct((8, TOK, 2 * COLS), jnp.float32),
         in_specs=[SM] * 2 + [VM] * 5,
         out_specs=VM,
         compiler_params=PARAMS,
@@ -169,7 +169,7 @@
     return jnp.where(col < limit, 0.0, -jnp.inf)
 
 
-def attend_kernel(lens_ref, part_ref, q_ref, k_ref, v_ref, o_ref):
+def attend_kernel(lens_ref, fresh_ref, q_ref, k_ref, v_ref, o_ref):
     old, new = PACK * CACHE, PACK * STEPS
     width, count = old + new, 8 * new
     scale = 1.4426950408889634 / HD**0.5
@@ -184,10 +184,7 @@
     for first in range(0, GROUPS, BATCH):
         units = []
         for i in range(first, first + BATCH):
-            fresh = part_ref[0, new * i : new * (i + 1), :].astype(jnp.float32)
-            for j in range(1, 8):
-                fresh = fresh + part_ref[j, new * i : new * (i + 1), :].astype(jnp.float32)
-            fresh = fresh.astype(jnp.bfloat16)
+            fresh = fresh_ref[new * i : new * (i + 1), :]
             rows = slice(PACK * i, PACK * (i + 1))
             past = slice(old * i, old * (i + 1))
             lens = [lens_ref[PACK * i + r] for r in range(PACK)]
@@ -229,7 +226,7 @@
                 o_ref[rows, :, h] = out[new * n : new * (n + 1)].reshape(PACK, STEPS, HD)
 
 
-def attend(lengths, parts, q, keys, values):
+def attend(lengths, fresh, q, keys, values):
     return pl.pallas_call(
         attend_kernel,
         out_shape=jax.ShapeDtypeStruct((ROWS, STEPS, FEAT), jnp.bfloat16),
@@ -237,7 +234,7 @@
         out_specs=VM,
         compiler_params=PARAMS,
         name="attend",
-    )(lengths, parts, q, keys, values)
+    )(lengths, fresh, q, keys, values)
 
 
 def flipped(x, axis):
@@ -267,11 +264,13 @@
     weight = lax.all_to_all(copies, FAR, 0, 0, tiled=True)
 
     partial = project(me, own, (features, beside, across, beyond), weight)
+    partial = (partial * 64.0).astype(jnp.float16)
     partial = lax.all_to_all(partial, CUBE, 0, 0, tiled=True)
+    fresh = (jnp.sum(partial.astype(jnp.float32), axis=0) * (1.0 / 64.0)).astype(jnp.bfloat16)
 
     keys = kv_cache[:, :, 0].reshape(ROWS * CACHE, COLS)
     values = kv_cache[:, :, 1].reshape(ROWS * CACHE, COLS)
-    context = attend(lengths, partial, queries, keys, values)
+    context = attend(lengths, fresh, queries, keys, values)
     return (new_master, new_one, new_two, context)
 
 

time: 110 us -> 111 us (level)
  other arithmetic: 0.05 us -> 1.92 us
  Pallas kernels: 10.8 us -> 9.63 us
    convert_element_type x0 -> x2, other arithmetic: none -> 1.65 us  [the longest x1 1.61 us: on_device(): partial = (partial * 64.0).astype(jnp.float16)]
    pallas_call x1, Pallas kernels: 4.16 us -> 2.99 us  [project(): pl.pallas_call(project_kernel, out_shape=jax.ShapeDtypeStruct((8, TOK, 2...]
where the time goes in v4:
time: 111 us; the launch traced here: 110 us
  starting transfers between devices  55.6 us (50%)
  waiting for transfers between devices  40.3 us (36%)
  Pallas kernels  9.63 us (9%)
  local copies, waits for them, and re-layouts  1.95 us (2%)
  other arithmetic  1.92 us (2%)
    all_to_all x1, waiting for transfers between devices, on_device(): partial = lax.all_to_all(partial, CUBE, 0, 0, tiled=True)  18.2 us
    ppermute x4, starting transfers between devices, flipped(): return lax.ppermute(x, axis, [(0, 1), (1, 0)])  17.5 us
    ppermute x4, waiting for transfers between devices, flipped(): return lax.ppermute(x, axis, [(0, 1), (1, 0)])  13 us
    all_to_all x1, starting transfers between devices, on_device(): weight = lax.all_to_all(copies, FAR, 0, 0, tiled=True)  11.6 us
    all_to_all x1, starting transfers between devices, on_device(): pieces = lax.all_to_all(pieces, FSDP, 0, 0, tiled=True)  10.9 us
    ppermute x3, starting transfers between devices, on_device(): lax.ppermute(pairs[p], ('yl', 'xl'), [(i, i ^ p) for i in range(4)])  8.37 us
    all_to_all x1, starting transfers between devices, on_device(): partial = lax.all_to_all(partial, CUBE, 0, 0, tiled=True)  7.3 us
    ppermute x3, waiting for transfers between devices, on_device(): lax.ppermute(pairs[p], ('yl', 'xl'), [(i, i ^ p) for i in range(4)])  5.69 us
  transfers between devices with their start and end apart: 10, of which 6 were waited for; matrix products, arithmetic and copies ran while one was open for 2% of the time, Pallas kernels for 2%

profile of v4, /device:TPU:1, one launch (start us, length us, event | category | flops | bytes accessed | tf_op | source)
XLA Modules:
  0.0 110.3 jit_solution(8113830972889188470)
XLA Ops:
  0.6 0.0 copy-start
  0.6 1.9 %by_owner.1 = bf16[8,2,64,256]{3,2,1,0:T(8,128)(2,1)} custom-call(bf16[1,2,8,64,256]{4,3,2,1,0:T(8,128)(2,1)} %bitcast.7), custom_call_target="tpu_custom_call" | custom-call | tf_op jit(solution)/shard_map/by_owner/pallas_call | solution.py:52
  2.6 10.9 %all-to-all-start = ((bf16[8,2,64,256]{3,2,1,0:T(8,128)(2,1)}), bf16[8,2,64,256]{3,2,1,0:T(8,128)(2,1)S(1)}, u32[]{:S(2)}, u32[]{:S(2)}) async-start(bf16[8,2,64,256]{3,2,1,0:T(8,128)(2,1)} %by_owner.1), calls=%async_computation | async-start | bytes 1048576 | tf_op jit(solution)/shard_map/all_to_all | solution.py:251
  13.4 0.0 copy-done
  13.4 0.0 copy-start.2
  13.5 0.0 copy-start.3
  13.5 0.0 copy-start.4
  13.5 0.4 split_features.1
  13.9 3.1 %collective-permute-start = (bf16[2,192,256]{2,1,0:T(8,128)(2,1)S(1)}, bf16[2,192,256]{2,1,0:T(8,128)(2,1)S(1)}, u32[]{:S(2)}, u32[]{:S(2)}) collective-permute-start(bf16[2,192,256]{2,1,0:T(8,128)(2,1)S(1)} %get-tuple-element.16), channel_id=1, source_target_pairs={{0,32},{32,0},{64,96},{96,64},{1,33},{33,1},{65,97},{97,65},{2,34}... | collective-permute-start | bytes 589832 | tf_op jit(solution)/shard_map/ppermute | solution.py:256
  17.0 3.2 %collective-permute-start.1 = (bf16[2,192,256]{2,1,0:T(8,128)(2,1)S(1)}, bf16[2,192,256]{2,1,0:T(8,128)(2,1)S(1)}, u32[]{:S(2)}, u32[]{:S(2)}) collective-permute-start(bf16[2,192,256]{2,1,0:T(8,128)(2,1)S(1)} %get-tuple-element.17), channel_id=1, source_target_pairs={{0,64},{32,96},{64,0},{96,32},{1,65},{33,97},{65,1},{97,33},{2,66}... | collective-permute-start | bytes 589832 | tf_op jit(solution)/shard_map/ppermute | solution.py:256
  20.3 2.0 %collective-permute-start.2 = (bf16[2,192,256]{2,1,0:T(8,128)(2,1)S(1)}, bf16[2,192,256]{2,1,0:T(8,128)(2,1)S(1)}, u32[]{:S(2)}, u32[]{:S(2)}) collective-permute-start(bf16[2,192,256]{2,1,0:T(8,128)(2,1)S(1)} %get-tuple-element.18), channel_id=1, source_target_pairs={{0,96},{32,64},{64,32},{96,0},{1,97},{33,65},{65,33},{97,1},{2,98}... | collective-permute-start | bytes 589832 | tf_op jit(solution)/shard_map/ppermute | solution.py:256
  22.3 0.0 collective-permute-done
  22.4 1.7 %collective-permute-done.1 = bf16[2,192,256]{2,1,0:T(8,128)(2,1)S(1)} collective-permute-done((bf16[2,192,256]{2,1,0:T(8,128)(2,1)S(1)}, bf16[2,192,256]{2,1,0:T(8,128)(2,1)S(1)}, u32[]{:S(2)}, u32[]{:S(2)}) %collective-permute-start.1) | collective-permute-done | bytes 196640 | tf_op jit(solution)/shard_map/ppermute | solution.py:256
  24.1 4.0 %collective-permute-done.2 = bf16[2,192,256]{2,1,0:T(8,128)(2,1)S(1)} collective-permute-done((bf16[2,192,256]{2,1,0:T(8,128)(2,1)S(1)}, bf16[2,192,256]{2,1,0:T(8,128)(2,1)S(1)}, u32[]{:S(2)}, u32[]{:S(2)}) %collective-permute-start.2) | collective-permute-done | bytes 196640 | tf_op jit(solution)/shard_map/ppermute | solution.py:256
  28.1 0.1 pad_maximum_fusion
  28.2 3.2 %collective-permute-start.3 = (bf16[4,192,256]{2,1,0:T(8,128)(2,1)S(1)}, bf16[4,192,256]{2,1,0:T(8,128)(2,1)S(1)}, u32[]{:S(2)}, u32[]{:S(2)}) collective-permute-start(bf16[4,192,256]{2,1,0:T(8,128)(2,1)S(1)} %pad_maximum_fusion), channel_id=1, source_target_pairs={{0,4},{4,0},{1,5},{5,1},{2,6},{6,2},{3,7},{7,3},{8,12},{12,8},{9,1... | collective-permute-start | bytes 1179656 | tf_op jit(solution)/shard_map/ppermute | solution.py:241
  31.4 0.0 all-to-all-done.g_ref
  31.4 0.0 copy-done.2
  31.4 0.0 copy-done.3
  31.4 0.0 copy-done.4
  31.4 1.3 %adamw.1 = (f32[2,64,256]{2,1,0:T(8,128)}, f32[2,64,256]{2,1,0:T(8,128)}, f32[2,64,256]{2,1,0:T(8,128)}, bf16[16,2,64,256]{3,2,1,0:T(8,128)(2,1)}) custom-call(bf16[8,2,64,256]{3,2,1,0:T(8,128)(2,1)S(1)} %all-to-all-done.g_ref, f32[2,64,256]{2,1,0:T(8,128)S(1)} %copy-done.2, f32[2,64,256]{2,1,0:T(8,128)S(1)} %copy-done.3, f32[2,64,256]{2,1,0:T(8,128)S(1)} %copy-done.4), custom_call_target="tpu_custom_call" | custom-call | tf_op jit(solution)/shard_map/adamw/pallas_call | solution.py:82
  32.7 11.6 %all-to-all-start.1 = ((bf16[16,2,64,256]{3,2,1,0:T(8,128)(2,1)}), bf16[16,2,64,256]{3,2,1,0:T(8,128)(2,1)S(1)}, u32[]{:S(2)}, u32[]{:S(2)}) async-start(bf16[16,2,64,256]{3,2,1,0:T(8,128)(2,1)} %get-tuple-element.19), calls=%async_computation.1 | async-start | bytes 2097152 | tf_op jit(solution)/shard_map/all_to_all | solution.py:264
  44.3 0.0 collective-permute-done.3
  44.4 4.7 %collective-permute-start.5 = (bf16[8,192,256]{2,1,0:T(8,128)(2,1)S(1)}, bf16[8,192,256]{2,1,0:T(8,128)(2,1)S(1)}, u32[]{:S(2)}, u32[]{:S(2)}) collective-permute-start(bf16[8,192,256]{2,1,0:T(8,128)(2,1)S(1)} %constant_dynamic-update-slice_fusion.xa), channel_id=1, source_target_pairs={{0,2},{2,0},{1,3},{3,1},{4,6},{6,4},{5,7},{7,5},{8,10},{10,8},{9,1... | collective-permute-start | bytes 2359304 | tf_op jit(solution)/shard_map/ppermute | solution.py:241
  49.1 4.4 %collective-permute-start.4 = (bf16[8,192,256]{2,1,0:T(8,128)(2,1)S(1)}, bf16[8,192,256]{2,1,0:T(8,128)(2,1)S(1)}, u32[]{:S(2)}, u32[]{:S(2)}) collective-permute-start(bf16[8,192,256]{2,1,0:T(8,128)(2,1)S(1)} %constant_dynamic-update-slice_fusion.xa), channel_id=1, source_target_pairs={{0,1},{1,0},{2,3},{3,2},{4,5},{5,4},{6,7},{7,6},{8,9},{9,8},{10,11... | collective-permute-start | bytes 2359304 | tf_op jit(solution)/shard_map/ppermute | solution.py:241
  53.5 11.0 %collective-permute-done.5.xc = bf16[8,192,256]{2,1,0:T(8,128)(2,1)S(1)} collective-permute-done((bf16[8,192,256]{2,1,0:T(8,128)(2,1)S(1)}, bf16[8,192,256]{2,1,0:T(8,128)(2,1)S(1)}, u32[]{:S(2)}, u32[]{:S(2)}) %collective-permute-start.5) | collective-permute-done | bytes 786464 | tf_op jit(solution)/shard_map/ppermute | solution.py:241
  64.5 5.1 %collective-permute-start.6 = (bf16[8,192,256]{2,1,0:T(8,128)(2,1)S(1)}, bf16[8,192,256]{2,1,0:T(8,128)(2,1)}, u32[]{:S(2)}, u32[]{:S(2)}) collective-permute-start(bf16[8,192,256]{2,1,0:T(8,128)(2,1)S(1)} %collective-permute-done.5.xc), channel_id=1, source_target_pairs={{0,1},{1,0},{2,3},{3,2},{4,5},{5,4},{6,7},{7,6},{8,9},{9,8},{10,11... | collective-permute-start | bytes 2359304 | tf_op jit(solution)/shard_map/ppermute | solution.py:241
  69.6 0.0 collective-permute-done.4.xb
  69.6 2.0 %collective-permute-done.6.xd = bf16[8,192,256]{2,1,0:T(8,128)(2,1)} collective-permute-done((bf16[8,192,256]{2,1,0:T(8,128)(2,1)S(1)}, bf16[8,192,256]{2,1,0:T(8,128)(2,1)}, u32[]{:S(2)}, u32[]{:S(2)}) %collective-permute-start.6) | collective-permute-done | bytes 786464 | tf_op jit(solution)/shard_map/ppermute | solution.py:241
  71.6 3.4 %all-to-all-done.1.w_ref = bf16[16,2,64,256]{3,2,1,0:T(8,128)(2,1)S(1)} async-done(((bf16[16,2,64,256]{3,2,1,0:T(8,128)(2,1)}), bf16[16,2,64,256]{3,2,1,0:T(8,128)(2,1)S(1)}, u32[]{:S(2)}, u32[]{:S(2)}) %all-to-all-start.1) | async-done | bytes 1048608 | tf_op jit(solution)/shard_map/all_to_all | solution.py:264
  75.0 3.0 %project.1 = f32[8,192,512]{2,1,0:T(8,128)S(1)} custom-call(s32[1]{0:T(128)} %bitcast.1.me_ref, s32[1]{0:T(128)} %bitcast.2.t_ref, bf16[8,192,256]{2,1,0:T(8,128)(2,1)S(1)} %constant_dynamic-update-slice_fusion.xa, bf16[8,192,256]{2,1,0:T(8,128)(2,1)S(1)} %collective-permute-done.4.xb, bf16[8,192,256]{2,1,0:T(8,128)(2,1)S(1)} %collective-permute-done.5.xc, ...), custom_call_target="tpu_custom_call" | custom-call | tf_op jit(solution)/shard_map/project/pallas_call | solution.py:141
  78.0 1.6 %multiply_convert_fusion = f16[8,192,512]{2,1,0:T(8,128)(2,1)} fusion(f32[8,192,512]{2,1,0:T(8,128)S(1)} %project.1), kind=kLoop, calls=%fused_computation.1 | loop fusion | flops 1572864 | bytes 4718592 | tf_op jit(solution)/shard_map/convert_element_type | solution.py:267
  79.6 0.0 copy-start.6
  79.6 7.3 %all-to-all-start.2 = ((f16[8,192,512]{2,1,0:T(8,128)(2,1)}), f16[8,192,512]{2,1,0:T(8,128)(2,1)S(1)}, u32[]{:S(2)}, u32[]{:S(2)}) async-start(f16[8,192,512]{2,1,0:T(8,128)(2,1)} %multiply_convert_fusion), calls=%async_computation.2 | async-start | bytes 3145728 | tf_op jit(solution)/shard_map/all_to_all | solution.py:268
  86.9 0.0 copy-done.6
  86.9 1.6 %fusion = (bf16[48,24,1,256]{3,2,1,0:T(2,128)(2,1)S(1)}, bf16[48,24,1,256]{3,2,1,0:T(2,128)(2,1)S(1)}) fusion(bf16[48,24,2,256]{3,2,1,0:T(2,128)(2,1)S(1)} %copy-done.6), kind=kLoop, calls=%fused_computation.9 | loop fusion | bytes 2359296 | tf_op jit(solution)/shard_map/slice | solution.py:272
  88.6 0.1 copy.15
  88.7 0.1 copy.14
  88.8 0.0 copy-start.1
  88.8 0.0 copy-start.5
  88.8 18.2 %all-to-all-done.2 = f16[8,192,512]{2,1,0:T(8,128)(2,1)S(1)} async-done(((f16[8,192,512]{2,1,0:T(8,128)(2,1)}), f16[8,192,512]{2,1,0:T(8,128)(2,1)S(1)}, u32[]{:S(2)}, u32[]{:S(2)}) %all-to-all-start.2) | async-done | bytes 1572896 | tf_op jit(solution)/shard_map/all_to_all | solution.py:268
  107.0 0.2 convert_reduce_fusion
  107.3 0.0 copy-done.1
  107.3 0.0 copy-done.5
  107.3 3.0 %attend.1 = bf16[48,4,2048]{2,1,0:T(4,128)(2,1)} custom-call(s32[48]{0:T(128)S(1)} %copy-done.5, bf16[192,512]{1,0:T(8,128)(2,1)S(1)} %multiply_convert_fusion.1.fresh_ref, bf16[48,4,2048]{2,1,0:T(4,128)(2,1)S(1)} %copy-done.1, bf16[1152,256]{1,0:T(8,128)(2,1)S(1)} %bitcast.6, bf16[1152,256]{1,0:T(8,128)(2,1)S(1)} %bitcast.5), custom_call_target="tpu_custom_call" | custom-call | tf_op jit(solution)/shard_map/attend/pallas_call | solution.py:230
  (6 shorter events, 0.1 us)
Async XLA Ops:
  0.6 12.8 %copy-start = (bf16[48,4,2048]{2,1,0:T(4,128)(2,1)S(1)}, bf16[48,4,2048]{2,1,0:T(4,128)(2,1)}, u32[]{:S(2)}) copy-start(bf16[48,4,2048]{2,1,0:T(4,128)(2,1)} %x_ref.1) | copy-start | bytes 2359300
  2.6 28.8 %all-to-all-start = ((bf16[8,2,64,256]{3,2,1,0:T(8,128)(2,1)}), bf16[8,2,64,256]{3,2,1,0:T(8,128)(2,1)S(1)}, u32[]{:S(2)}, u32[]{:S(2)}) async-start(bf16[8,2,64,256]{3,2,1,0:T(8,128)(2,1)} %by_owner.1), calls=%async_computation | async-start | bytes 1048576 | tf_op jit(solution)/shard_map/all_to_all | solution.py:251
  13.4 18.0 %copy-start.2 = (f32[2,64,256]{2,1,0:T(8,128)S(1)}, f32[2,64,256]{2,1,0:T(8,128)}, u32[]{:S(2)}) copy-start(f32[2,64,256]{2,1,0:T(8,128)} %w_ref.1) | copy-start | bytes 393220
  13.5 17.9 %copy-start.3 = (f32[2,64,256]{2,1,0:T(8,128)S(1)}, f32[2,64,256]{2,1,0:T(8,128)}, u32[]{:S(2)}) copy-start(f32[2,64,256]{2,1,0:T(8,128)} %one_ref.1) | copy-start | bytes 393220
  13.5 17.9 %copy-start.4 = (f32[2,64,256]{2,1,0:T(8,128)S(1)}, f32[2,64,256]{2,1,0:T(8,128)}, u32[]{:S(2)}) copy-start(f32[2,64,256]{2,1,0:T(8,128)} %two_ref.1) | copy-start | bytes 393220
  13.9 8.4 %collective-permute-start = (bf16[2,192,256]{2,1,0:T(8,128)(2,1)S(1)}, bf16[2,192,256]{2,1,0:T(8,128)(2,1)S(1)}, u32[]{:S(2)}, u32[]{:S(2)}) collective-permute-start(bf16[2,192,256]{2,1,0:T(8,128)(2,1)S(1)} %get-tuple-element.16), channel_id=1, source_target_pairs={{0,32},{32,0},{64,96},{96,64},{1,33},{33,1},{65,97},{97,65},{2,34}... | collective-permute-start | bytes 589832 | tf_op jit(solution)/shard_map/ppermute | solution.py:256
  17.0 7.0 %collective-permute-start.1 = (bf16[2,192,256]{2,1,0:T(8,128)(2,1)S(1)}, bf16[2,192,256]{2,1,0:T(8,128)(2,1)S(1)}, u32[]{:S(2)}, u32[]{:S(2)}) collective-permute-start(bf16[2,192,256]{2,1,0:T(8,128)(2,1)S(1)} %get-tuple-element.17), channel_id=1, source_target_pairs={{0,64},{32,96},{64,0},{96,32},{1,65},{33,97},{65,1},{97,33},{2,66}... | collective-permute-start | bytes 589832 | tf_op jit(solution)/shard_map/ppermute | solution.py:256
  20.3 7.8 %collective-permute-start.2 = (bf16[2,192,256]{2,1,0:T(8,128)(2,1)S(1)}, bf16[2,192,256]{2,1,0:T(8,128)(2,1)S(1)}, u32[]{:S(2)}, u32[]{:S(2)}) collective-permute-start(bf16[2,192,256]{2,1,0:T(8,128)(2,1)S(1)} %get-tuple-element.18), channel_id=1, source_target_pairs={{0,96},{32,64},{64,32},{96,0},{1,97},{33,65},{65,33},{97,1},{2,98}... | collective-permute-start | bytes 589832 | tf_op jit(solution)/shard_map/ppermute | solution.py:256
  28.2 16.2 %collective-permute-start.3 = (bf16[4,192,256]{2,1,0:T(8,128)(2,1)S(1)}, bf16[4,192,256]{2,1,0:T(8,128)(2,1)S(1)}, u32[]{:S(2)}, u32[]{:S(2)}) collective-permute-start(bf16[4,192,256]{2,1,0:T(8,128)(2,1)S(1)} %pad_maximum_fusion), channel_id=1, source_target_pairs={{0,4},{4,0},{1,5},{5,1},{2,6},{6,2},{3,7},{7,3},{8,12},{12,8},{9,1... | collective-permute-start | bytes 1179656 | tf_op jit(solution)/shard_map/ppermute | solution.py:241
  32.7 42.3 %all-to-all-start.1 = ((bf16[16,2,64,256]{3,2,1,0:T(8,128)(2,1)}), bf16[16,2,64,256]{3,2,1,0:T(8,128)(2,1)S(1)}, u32[]{:S(2)}, u32[]{:S(2)}) async-start(bf16[16,2,64,256]{3,2,1,0:T(8,128)(2,1)} %get-tuple-element.19), calls=%async_computation.1 | async-start | bytes 2097152 | tf_op jit(solution)/shard_map/all_to_all | solution.py:264
  44.4 20.1 %collective-permute-start.5 = (bf16[8,192,256]{2,1,0:T(8,128)(2,1)S(1)}, bf16[8,192,256]{2,1,0:T(8,128)(2,1)S(1)}, u32[]{:S(2)}, u32[]{:S(2)}) collective-permute-start(bf16[8,192,256]{2,1,0:T(8,128)(2,1)S(1)} %constant_dynamic-update-slice_fusion.xa), channel_id=1, source_target_pairs={{0,2},{2,0},{1,3},{3,1},{4,6},{6,4},{5,7},{7,5},{8,10},{10,8},{9,1... | collective-permute-start | bytes 2359304 | tf_op jit(solution)/shard_map/ppermute | solution.py:241
  49.1 20.5 %collective-permute-start.4 = (bf16[8,192,256]{2,1,0:T(8,128)(2,1)S(1)}, bf16[8,192,256]{2,1,0:T(8,128)(2,1)S(1)}, u32[]{:S(2)}, u32[]{:S(2)}) collective-permute-start(bf16[8,192,256]{2,1,0:T(8,128)(2,1)S(1)} %constant_dynamic-update-slice_fusion.xa), channel_id=1, source_target_pairs={{0,1},{1,0},{2,3},{3,2},{4,5},{5,4},{6,7},{7,6},{8,9},{9,8},{10,11... | collective-permute-start | bytes 2359304 | tf_op jit(solution)/shard_map/ppermute | solution.py:241
  64.5 7.2 %collective-permute-start.6 = (bf16[8,192,256]{2,1,0:T(8,128)(2,1)S(1)}, bf16[8,192,256]{2,1,0:T(8,128)(2,1)}, u32[]{:S(2)}, u32[]{:S(2)}) collective-permute-start(bf16[8,192,256]{2,1,0:T(8,128)(2,1)S(1)} %collective-permute-done.5.xc), channel_id=1, source_target_pairs={{0,1},{1,0},{2,3},{3,2},{4,5},{5,4},{6,7},{7,6},{8,9},{9,8},{10,11... | collective-permute-start | bytes 2359304 | tf_op jit(solution)/shard_map/ppermute | solution.py:241
  79.6 7.3 %copy-start.6 = (bf16[48,24,2,256]{3,2,1,0:T(2,128)(2,1)S(1)}, bf16[48,24,2,256]{3,2,1,0:T(2,128)(2,1)}, u32[]{:S(2)}) copy-start(bf16[48,24,2,256]{3,2,1,0:T(2,128)(2,1)} %param.14) | copy-start | bytes 3538948
  79.6 27.4 %all-to-all-start.2 = ((f16[8,192,512]{2,1,0:T(8,128)(2,1)}), f16[8,192,512]{2,1,0:T(8,128)(2,1)S(1)}, u32[]{:S(2)}, u32[]{:S(2)}) async-start(f16[8,192,512]{2,1,0:T(8,128)(2,1)} %multiply_convert_fusion), calls=%async_computation.2 | async-start | bytes 3145728 | tf_op jit(solution)/shard_map/all_to_all | solution.py:268
  88.8 18.5 %copy-start.1 = (bf16[48,4,2048]{2,1,0:T(4,128)(2,1)S(1)}, bf16[48,4,2048]{2,1,0:T(4,128)(2,1)}, u32[]{:S(2)}) copy-start(bf16[48,4,2048]{2,1,0:T(4,128)(2,1)} %q_ref.1) | copy-start | bytes 2359300
  88.8 18.5 %copy-start.5 = (s32[48]{0:T(128)S(1)}, s32[48]{0:T(128)}, u32[]{:S(2)}) copy-start(s32[48]{0:T(128)} %lens_ref.1) | copy-start | bytes 580

commit v5 on v4

--- a/solution.py
+++ b/solution.py
@@ -89,8 +89,7 @@
     )(pieces, master, moment_one, moment_two)
 
 
-def split_kernel(me_ref, x_ref, *refs):
-    blocks = refs[4]
+def split_kernel(me_ref, x_ref, kept_ref, sent_ref, blocks):
     for b in range(4):
         v = [
             x_ref[:, :, 512 * b + 128 * k : 512 * b + 128 * (k + 1)].reshape(TOK, 128)
@@ -102,46 +101,50 @@
                 blocks[2 * b + half, :, 128 * p : 128 * (p + 1)] = jnp.concatenate(
                     [v[2 * p][:, cut], v[2 * p + 1][:, cut]], axis=1
                 )
-    for p in range(4):
-        for d in range(2):
-            refs[p][d] = blocks[me_ref[0] ^ (2 * p + d)]
+    for d in range(4):
+        away = d // 2 + 2 * (d % 2)
+        kept_ref[d] = blocks[me_ref[0] ^ away]
+        sent_ref[d] = blocks[me_ref[0] ^ away ^ 4]
 
 
 def split_features(me, x):
-    pair = jax.ShapeDtypeStruct((2, TOK, COLS), jnp.bfloat16)
+    half = jax.ShapeDtypeStruct((4, TOK, COLS), jnp.bfloat16)
     return pl.pallas_call(
         split_kernel,
-        out_shape=(pair,) * 4,
+        out_shape=(half, half),
         in_specs=[SM, VM],
-        out_specs=(VM,) * 4,
+        out_specs=(VM, VM),
         scratch_shapes=[pltpu.VMEM((8, TOK, COLS), jnp.bfloat16)],
         compiler_params=PARAMS,
         name="split_features",
     )(me, x)
 
 
-def project_kernel(me_ref, t_ref, xa, xb, xc, xd, w_ref, o_ref):
+def project_kernel(me_ref, t_ref, *refs):
+    w_ref, o_ref = refs[8], refs[9]
     me, own = me_ref[0], t_ref[0]
     for kv in range(2):
         w = jnp.concatenate(
             [w_ref[pl.ds(4 * (own ^ f), 4), kv].reshape(COLS, COLS) for f in range(4)], axis=0
         )
-        for m in range(0, 8, 2):
-            x = jnp.concatenate(
-                [r[m : m + 2].reshape(2 * TOK, COLS) for r in (xa, xb, xc, xd)], axis=1
-            )
-            y = jnp.dot(x, w, preferred_element_type=jnp.float32)
-            for d in range(m, m + 2):
-                o_ref[me ^ (2 * (d % 4) + d // 4), :, kv * COLS : (kv + 1) * COLS] = y[
-                    TOK * (d - m) : TOK * (d - m + 1)
-                ]
+        for half in range(2):
+            for m in range(0, 4, 2):
+                x = jnp.concatenate(
+                    [refs[2 * f + half][m : m + 2].reshape(2 * TOK, COLS) for f in range(4)],
+                    axis=1,
+                )
+                y = jnp.dot(x, w, preferred_element_type=jnp.float32)
+                for d in range(2):
+                    o_ref[me ^ (m // 2 + 4 * d + 2 * half), :, kv * COLS : (kv + 1) * COLS] = y[
+                        TOK * d : TOK * (d + 1)
+                    ]
 
 
 def project(me, own, features, w):
     return pl.pallas_call(
         project_kernel,
         out_shape=jax.ShapeDtypeStruct((8, TOK, 2 * COLS), jnp.float32),
-        in_specs=[SM] * 2 + [VM] * 5,
+        in_specs=[SM] * 2 + [VM] * 9,
         out_specs=VM,
         compiler_params=PARAMS,
         name="project",
@@ -251,19 +254,20 @@
     pieces = lax.all_to_all(pieces, FSDP, 0, 0, tiled=True)
     new_master, new_one, new_two, copies = adamw(pieces, master_weight, moment_one, moment_two)
 
-    pairs = split_features(me, layer_inputs)
-    pairs = [pairs[0]] + [
-        lax.ppermute(pairs[p], ("yl", "xl"), [(i, i ^ p) for i in range(4)]) for p in range(1, 4)
-    ]
-    far = flipped(jnp.concatenate([pair[1:2] for pair in pairs]), "zl")
-    features = jnp.concatenate([pair[0:1] for pair in pairs] + [far])
-    beside = flipped(features, "c")
-    across = flipped(features, "xh")
-    beyond = flipped(across, "c")
+    kept, sent = split_features(me, layer_inputs)
+    by_y = flipped(sent, "yl")
+    by_z = flipped(jnp.concatenate([kept[2:4], by_y[2:4]]), "zl")
+    near = jnp.concatenate([kept[0:1], by_y[0:1], by_z[0:1], by_z[2:3]])
+    far = flipped(jnp.concatenate([kept[1:2], by_y[1:2], by_z[1:2], by_z[3:4]]), "xl")
+    features = []
+    for half in (near, far):
+        across = flipped(half, "xh")
+        features.append((half, flipped(half, "c"), across, flipped(across, "c")))
+    features = [features[h][f] for f in range(4) for h in range(2)]
 
     weight = lax.all_to_all(copies, FAR, 0, 0, tiled=True)
 
-    partial = project(me, own, (features, beside, across, beyond), weight)
+    partial = project(me, own, features, weight)
     partial = (partial * 64.0).astype(jnp.float16)
     partial = lax.all_to_all(partial, CUBE, 0, 0, tiled=True)
     fresh = (jnp.sum(partial.astype(jnp.float32), axis=0) * (1.0 / 64.0)).astype(jnp.bfloat16)

time: 111 us -> 109 us (0.982)
  waiting for transfers between devices: 40.3 us -> 33 us
  starting transfers between devices: 55.6 us -> 61.1 us
    ppermute x4 -> x9, starting transfers between devices: 17.5 us -> 38.3 us  [flipped(): return lax.ppermute(x, axis, [(0, 1), (1, 0)])]
    ppermute x3 -> x0, starting transfers between devices: 8.37 us -> none  [on_device(): lax.ppermute(pairs[p], ('yl', 'xl'), [(i, i ^ p) for i in range(4)])]
    ppermute x3 -> x0, waiting for transfers between devices: 5.69 us -> none  [on_device(): lax.ppermute(pairs[p], ('yl', 'xl'), [(i, i ^ p) for i in range(4)])]
    all_to_all x1, starting transfers between devices: 7.3 us -> 3.71 us  [on_device(): partial = lax.all_to_all(partial, CUBE, 0, 0, tiled=True)]
    all_to_all x1, starting transfers between devices: 11.6 us -> 8.04 us  [on_device(): weight = lax.all_to_all(copies, FAR, 0, 0, tiled=True)]
    all_to_all x1, waiting for transfers between devices: 3.38 us -> 0.01 us  [on_device(): weight = lax.all_to_all(copies, FAR, 0, 0, tiled=True)]
    all_to_all x1, waiting for transfers between devices: 0.02 us -> 2.82 us  [on_device(): pieces = lax.all_to_all(pieces, FSDP, 0, 0, tiled=True)]
    ppermute x4 -> x9, waiting for transfers between devices: 13 us -> 12 us  [flipped(): return lax.ppermute(x, axis, [(0, 1), (1, 0)])]
  transfers between devices with their start and end apart: 10 -> 12, of which waited for: 6 -> 5; matrix products, arithmetic and copies ran while one was open for 2% -> 2% of each run, Pallas kernels for 2% -> 2%
where the time goes in v5:
time: 109 us
  starting transfers between devices  61.1 us (56%)
  waiting for transfers between devices  33 us (30%)
  Pallas kernels  9.63 us (9%)
  other arithmetic  2 us (2%)
  local copies, waits for them, and re-layouts  1.95 us (2%)
    ppermute x9, starting transfers between devices, flipped(): return lax.ppermute(x, axis, [(0, 1), (1, 0)])  38.3 us
    all_to_all x1, waiting for transfers between devices, on_device(): partial = lax.all_to_all(partial, CUBE, 0, 0, tiled=True)  18.2 us
    ppermute x9, waiting for transfers between devices, flipped(): return lax.ppermute(x, axis, [(0, 1), (1, 0)])  12 us
    all_to_all x1, starting transfers between devices, on_device(): pieces = lax.all_to_all(pieces, FSDP, 0, 0, tiled=True)  11 us
    all_to_all x1, starting transfers between devices, on_device(): weight = lax.all_to_all(copies, FAR, 0, 0, tiled=True)  8.04 us
    all_to_all x1, starting transfers between devices, on_device(): partial = lax.all_to_all(partial, CUBE, 0, 0, tiled=True)  3.71 us
    pallas_call x1, Pallas kernels, attend(): pl.pallas_call(attend_kernel, out_shape=jax.ShapeDtypeStruct((ROWS, STEPS...  3 us
    pallas_call x1, Pallas kernels, project(): pl.pallas_call(project_kernel, out_shape=jax.ShapeDtypeStruct((8, TOK, 2...  2.98 us
  transfers between devices with their start and end apart: 12, of which 5 were waited for; matrix products, arithmetic and copies ran while one was open for 2% of the time, Pallas kernels for 2%

profile of v5, /device:TPU:1, one launch (start us, length us, event | category | flops | bytes accessed | tf_op | source)
XLA Modules:
  0.0 108.6 jit_solution(8702595415093291564)
XLA Ops:
  0.6 0.0 copy-start
  0.6 1.9 %by_owner.1 = bf16[8,2,64,256]{3,2,1,0:T(8,128)(2,1)} custom-call(bf16[1,2,8,64,256]{4,3,2,1,0:T(8,128)(2,1)} %bitcast.7), custom_call_target="tpu_custom_call" | custom-call | tf_op jit(solution)/shard_map/by_owner/pallas_call | solution.py:52
  2.6 0.0 copy-start.2
  2.6 0.0 copy-start.3
  2.6 0.0 copy-start.4
  2.6 11.0 %all-to-all-start = ((bf16[8,2,64,256]{3,2,1,0:T(8,128)(2,1)}), bf16[8,2,64,256]{3,2,1,0:T(8,128)(2,1)S(1)}, u32[]{:S(2)}, u32[]{:S(2)}) async-start(bf16[8,2,64,256]{3,2,1,0:T(8,128)(2,1)} %by_owner.1), calls=%async_computation | async-start | bytes 1048576 | tf_op jit(solution)/shard_map/all_to_all | solution.py:254
  13.6 0.0 copy-done
  13.6 0.4 split_features.1
  14.0 3.2 %collective-permute-start = (bf16[4,192,256]{2,1,0:T(8,128)(2,1)S(1)}, bf16[4,192,256]{2,1,0:T(8,128)(2,1)S(1)}, u32[]{:S(2)}, u32[]{:S(2)}) collective-permute-start(bf16[4,192,256]{2,1,0:T(8,128)(2,1)S(1)} %get-tuple-element.14), channel_id=1, source_target_pairs={{0,64},{64,0},{1,65},{65,1},{2,66},{66,2},{3,67},{67,3},{4,68},{68... | collective-permute-start | bytes 1179656 | tf_op jit(solution)/shard_map/ppermute | solution.py:244
  17.3 8.3 %collective-permute-done = bf16[4,192,256]{2,1,0:T(8,128)(2,1)S(1)} collective-permute-done((bf16[4,192,256]{2,1,0:T(8,128)(2,1)S(1)}, bf16[4,192,256]{2,1,0:T(8,128)(2,1)S(1)}, u32[]{:S(2)}, u32[]{:S(2)}) %collective-permute-start) | collective-permute-done | bytes 393248 | tf_op jit(solution)/shard_map/ppermute | solution.py:244
  25.7 3.1 %collective-permute-start.1 = (bf16[4,192,256]{2,1,0:T(8,128)(2,1)S(1)}, bf16[4,192,256]{2,1,0:T(8,128)(2,1)S(1)}, u32[]{:S(2)}, u32[]{:S(2)}) collective-permute-start(bf16[4,192,256]{2,1,0:T(8,128)(2,1)S(1)} %pad_maximum_fusion), channel_id=1, source_target_pairs={{0,4},{4,0},{1,5},{5,1},{2,6},{6,2},{3,7},{7,3},{8,12},{12,8},{9,1... | collective-permute-start | bytes 1179656 | tf_op jit(solution)/shard_map/ppermute | solution.py:244
  28.7 2.8 %all-to-all-done.g_ref = bf16[8,2,64,256]{3,2,1,0:T(8,128)(2,1)S(1)} async-done(((bf16[8,2,64,256]{3,2,1,0:T(8,128)(2,1)}), bf16[8,2,64,256]{3,2,1,0:T(8,128)(2,1)S(1)}, u32[]{:S(2)}, u32[]{:S(2)}) %all-to-all-start) | async-done | bytes 524320 | tf_op jit(solution)/shard_map/all_to_all | solution.py:254
  31.6 0.0 copy-done.2
  31.6 0.0 copy-done.3
  31.6 0.0 copy-done.4
  31.6 1.3 %adamw.1 = (f32[2,64,256]{2,1,0:T(8,128)}, f32[2,64,256]{2,1,0:T(8,128)}, f32[2,64,256]{2,1,0:T(8,128)}, bf16[16,2,64,256]{3,2,1,0:T(8,128)(2,1)}) custom-call(bf16[8,2,64,256]{3,2,1,0:T(8,128)(2,1)S(1)} %all-to-all-done.g_ref, f32[2,64,256]{2,1,0:T(8,128)S(1)} %copy-done.2, f32[2,64,256]{2,1,0:T(8,128)S(1)} %copy-done.3, f32[2,64,256]{2,1,0:T(8,128)S(1)} %copy-done.4), custom_call_target="tpu_custom_call" | custom-call | tf_op jit(solution)/shard_map/adamw/pallas_call | solution.py:82
  32.9 8.0 %all-to-all-start.1 = ((bf16[16,2,64,256]{3,2,1,0:T(8,128)(2,1)}), bf16[16,2,64,256]{3,2,1,0:T(8,128)(2,1)S(1)}, u32[]{:S(2)}, u32[]{:S(2)}) async-start(bf16[16,2,64,256]{3,2,1,0:T(8,128)(2,1)} %get-tuple-element.15), calls=%async_computation.1 | async-start | bytes 2097152 | tf_op jit(solution)/shard_map/all_to_all | solution.py:268
  41.0 0.0 collective-permute-done.1
  41.0 0.1 pad_maximum_fusion.2
  41.1 3.1 %collective-permute-start.2 = (bf16[4,192,256]{2,1,0:T(8,128)(2,1)S(1)}, bf16[4,192,256]{2,1,0:T(8,128)(2,1)S(1)}, u32[]{:S(2)}, u32[]{:S(2)}) collective-permute-start(bf16[4,192,256]{2,1,0:T(8,128)(2,1)S(1)} %pad_maximum_fusion.2), channel_id=1, source_target_pairs={{0,32},{32,0},{1,33},{33,1},{2,34},{34,2},{3,35},{35,3},{4,36},{36... | collective-permute-start | bytes 1179656 | tf_op jit(solution)/shard_map/ppermute | solution.py:244
  44.2 0.1 pad_maximum_fusion.1.refs_0_
  44.3 4.4 %collective-permute-start.5 = (bf16[4,192,256]{2,1,0:T(8,128)(2,1)S(1)}, bf16[4,192,256]{2,1,0:T(8,128)(2,1)S(1)}, u32[]{:S(2)}, u32[]{:S(2)}) collective-permute-start(bf16[4,192,256]{2,1,0:T(8,128)(2,1)S(1)} %pad_maximum_fusion.1.refs_0_), channel_id=1, source_target_pairs={{0,2},{2,0},{1,3},{3,1},{4,6},{6,4},{5,7},{7,5},{8,10},{10,8},{9,1... | collective-permute-start | bytes 1179656 | tf_op jit(solution)/shard_map/ppermute | solution.py:244
  48.6 2.2 %collective-permute-done.2.refs_1_ = bf16[4,192,256]{2,1,0:T(8,128)(2,1)S(1)} collective-permute-done((bf16[4,192,256]{2,1,0:T(8,128)(2,1)S(1)}, bf16[4,192,256]{2,1,0:T(8,128)(2,1)S(1)}, u32[]{:S(2)}, u32[]{:S(2)}) %collective-permute-start.2) | collective-permute-done | bytes 393248 | tf_op jit(solution)/shard_map/ppermute | solution.py:244
  50.9 4.6 %collective-permute-start.6 = (bf16[4,192,256]{2,1,0:T(8,128)(2,1)S(1)}, bf16[4,192,256]{2,1,0:T(8,128)(2,1)S(1)}, u32[]{:S(2)}, u32[]{:S(2)}) collective-permute-start(bf16[4,192,256]{2,1,0:T(8,128)(2,1)S(1)} %collective-permute-done.2.refs_1_), channel_id=1, source_target_pairs={{0,2},{2,0},{1,3},{3,1},{4,6},{6,4},{5,7},{7,5},{8,10},{10,8},{9,1... | collective-permute-start | bytes 1179656 | tf_op jit(solution)/shard_map/ppermute | solution.py:244
  55.5 9.1 %collective-permute-start.3 = (bf16[4,192,256]{2,1,0:T(8,128)(2,1)S(1)}, bf16[4,192,256]{2,1,0:T(8,128)(2,1)S(1)}, u32[]{:S(2)}, u32[]{:S(2)}) collective-permute-start(bf16[4,192,256]{2,1,0:T(8,128)(2,1)S(1)} %pad_maximum_fusion.1.refs_0_), channel_id=1, source_target_pairs={{0,1},{1,0},{2,3},{3,2},{4,5},{5,4},{6,7},{7,6},{8,9},{9,8},{10,11... | collective-permute-start | bytes 1179656 | tf_op jit(solution)/shard_map/ppermute | solution.py:244
  64.6 1.9 %collective-permute-start.4 = (bf16[4,192,256]{2,1,0:T(8,128)(2,1)S(1)}, bf16[4,192,256]{2,1,0:T(8,128)(2,1)S(1)}, u32[]{:S(2)}, u32[]{:S(2)}) collective-permute-start(bf16[4,192,256]{2,1,0:T(8,128)(2,1)S(1)} %collective-permute-done.2.refs_1_), channel_id=1, source_target_pairs={{0,1},{1,0},{2,3},{3,2},{4,5},{5,4},{6,7},{7,6},{8,9},{9,8},{10,11... | collective-permute-start | bytes 1179656 | tf_op jit(solution)/shard_map/ppermute | solution.py:244
  66.5 0.0 collective-permute-done.5.refs_4_
  66.5 3.7 %collective-permute-start.7 = (bf16[4,192,256]{2,1,0:T(8,128)(2,1)S(1)}, bf16[4,192,256]{2,1,0:T(8,128)(2,1)}, u32[]{:S(2)}, u32[]{:S(2)}) collective-permute-start(bf16[4,192,256]{2,1,0:T(8,128)(2,1)S(1)} %collective-permute-done.5.refs_4_), channel_id=1, source_target_pairs={{0,1},{1,0},{2,3},{3,2},{4,5},{5,4},{6,7},{7,6},{8,9},{9,8},{10,11... | collective-permute-start | bytes 1179656 | tf_op jit(solution)/shard_map/ppermute | solution.py:244
  70.3 0.0 collective-permute-done.6.refs_5_
  70.3 5.2 %collective-permute-start.8 = (bf16[4,192,256]{2,1,0:T(8,128)(2,1)S(1)}, bf16[4,192,256]{2,1,0:T(8,128)(2,1)}, u32[]{:S(2)}, u32[]{:S(2)}) collective-permute-start(bf16[4,192,256]{2,1,0:T(8,128)(2,1)S(1)} %collective-permute-done.6.refs_5_), channel_id=1, source_target_pairs={{0,1},{1,0},{2,3},{3,2},{4,5},{5,4},{6,7},{7,6},{8,9},{9,8},{10,11... | collective-permute-start | bytes 1179656 | tf_op jit(solution)/shard_map/ppermute | solution.py:244
  75.5 0.0 collective-permute-done.3.refs_2_
  75.5 0.0 collective-permute-done.7.refs_6_
  75.5 0.0 collective-permute-done.4.refs_3_
  75.5 1.4 %collective-permute-done.8.refs_7_ = bf16[4,192,256]{2,1,0:T(8,128)(2,1)} collective-permute-done((bf16[4,192,256]{2,1,0:T(8,128)(2,1)S(1)}, bf16[4,192,256]{2,1,0:T(8,128)(2,1)}, u32[]{:S(2)}, u32[]{:S(2)}) %collective-permute-start.8) | collective-permute-done | bytes 393248 | tf_op jit(solution)/shard_map/ppermute | solution.py:244
  76.9 0.0 all-to-all-done.1.refs_8_
  76.9 3.0 %project.1 = f32[8,192,512]{2,1,0:T(8,128)S(1)} custom-call(s32[1]{0:T(128)} %bitcast.1.me_ref, s32[1]{0:T(128)} %bitcast.2.t_ref, bf16[4,192,256]{2,1,0:T(8,128)(2,1)S(1)} %pad_maximum_fusion.1.refs_0_, bf16[4,192,256]{2,1,0:T(8,128)(2,1)S(1)} %collective-permute-done.2.refs_1_, bf16[4,192,256]{2,1,0:T(8,128)(2,1)S(1)} %collective-permute-done.3.refs_2_, ...), custom_call_target="tpu_custom_call" | custom-call | tf_op jit(solution)/shard_map/project/pallas_call | solution.py:144
  79.9 1.6 %multiply_convert_fusion = f16[8,192,512]{2,1,0:T(8,128)(2,1)} fusion(f32[8,192,512]{2,1,0:T(8,128)S(1)} %project.1), kind=kLoop, calls=%fused_computation.1 | loop fusion | flops 1572864 | bytes 4718592 | tf_op jit(solution)/shard_map/convert_element_type | solution.py:271
  81.5 0.0 copy-start.6
  81.5 3.7 %all-to-all-start.2 = ((f16[8,192,512]{2,1,0:T(8,128)(2,1)}), f16[8,192,512]{2,1,0:T(8,128)(2,1)S(1)}, u32[]{:S(2)}, u32[]{:S(2)}) async-start(f16[8,192,512]{2,1,0:T(8,128)(2,1)} %multiply_convert_fusion), calls=%async_computation.2 | async-start | bytes 3145728 | tf_op jit(solution)/shard_map/all_to_all | solution.py:272
  85.2 0.0 copy-done.6
  85.3 1.6 %fusion = (bf16[48,24,1,256]{3,2,1,0:T(2,128)(2,1)S(1)}, bf16[48,24,1,256]{3,2,1,0:T(2,128)(2,1)S(1)}) fusion(bf16[48,24,2,256]{3,2,1,0:T(2,128)(2,1)S(1)} %copy-done.6), kind=kLoop, calls=%fused_computation.6 | loop fusion | bytes 2359296 | tf_op jit(solution)/shard_map/slice | solution.py:276
  86.9 0.1 copy.15
  87.0 0.1 copy.14
  87.1 0.0 copy-start.1
  87.1 0.0 copy-start.5
  87.1 18.2 %all-to-all-done.2 = f16[8,192,512]{2,1,0:T(8,128)(2,1)S(1)} async-done(((f16[8,192,512]{2,1,0:T(8,128)(2,1)}), f16[8,192,512]{2,1,0:T(8,128)(2,1)S(1)}, u32[]{:S(2)}, u32[]{:S(2)}) %all-to-all-start.2) | async-done | bytes 1572896 | tf_op jit(solution)/shard_map/all_to_all | solution.py:272
  105.3 0.2 convert_reduce_fusion
  105.5 0.0 copy-done.1
  105.5 0.0 copy-done.5
  105.6 3.0 %attend.1 = bf16[48,4,2048]{2,1,0:T(4,128)(2,1)} custom-call(s32[48]{0:T(128)S(1)} %copy-done.5, bf16[192,512]{1,0:T(8,128)(2,1)S(1)} %multiply_convert_fusion.1.fresh_ref, bf16[48,4,2048]{2,1,0:T(4,128)(2,1)S(1)} %copy-done.1, bf16[1152,256]{1,0:T(8,128)(2,1)S(1)} %bitcast.6, bf16[1152,256]{1,0:T(8,128)(2,1)S(1)} %bitcast.5), custom_call_target="tpu_custom_call" | custom-call | tf_op jit(solution)/shard_map/attend/pallas_call | solution.py:233
  (7 shorter events, 0.2 us)
Async XLA Ops:
  0.6 13.0 %copy-start = (bf16[48,4,2048]{2,1,0:T(4,128)(2,1)S(1)}, bf16[48,4,2048]{2,1,0:T(4,128)(2,1)}, u32[]{:S(2)}) copy-start(bf16[48,4,2048]{2,1,0:T(4,128)(2,1)} %x_ref.1) | copy-start | bytes 2359300
  2.6 29.0 %copy-start.2 = (f32[2,64,256]{2,1,0:T(8,128)S(1)}, f32[2,64,256]{2,1,0:T(8,128)}, u32[]{:S(2)}) copy-start(f32[2,64,256]{2,1,0:T(8,128)} %w_ref.1) | copy-start | bytes 393220
  2.6 29.0 %copy-start.3 = (f32[2,64,256]{2,1,0:T(8,128)S(1)}, f32[2,64,256]{2,1,0:T(8,128)}, u32[]{:S(2)}) copy-start(f32[2,64,256]{2,1,0:T(8,128)} %one_ref.1) | copy-start | bytes 393220
  2.6 29.0 %copy-start.4 = (f32[2,64,256]{2,1,0:T(8,128)S(1)}, f32[2,64,256]{2,1,0:T(8,128)}, u32[]{:S(2)}) copy-start(f32[2,64,256]{2,1,0:T(8,128)} %two_ref.1) | copy-start | bytes 393220
  2.6 29.0 %all-to-all-start = ((bf16[8,2,64,256]{3,2,1,0:T(8,128)(2,1)}), bf16[8,2,64,256]{3,2,1,0:T(8,128)(2,1)S(1)}, u32[]{:S(2)}, u32[]{:S(2)}) async-start(bf16[8,2,64,256]{3,2,1,0:T(8,128)(2,1)} %by_owner.1), calls=%async_computation | async-start | bytes 1048576 | tf_op jit(solution)/shard_map/all_to_all | solution.py:254
  14.0 11.6 %collective-permute-start = (bf16[4,192,256]{2,1,0:T(8,128)(2,1)S(1)}, bf16[4,192,256]{2,1,0:T(8,128)(2,1)S(1)}, u32[]{:S(2)}, u32[]{:S(2)}) collective-permute-start(bf16[4,192,256]{2,1,0:T(8,128)(2,1)S(1)} %get-tuple-element.14), channel_id=1, source_target_pairs={{0,64},{64,0},{1,65},{65,1},{2,66},{66,2},{3,67},{67,3},{4,68},{68... | collective-permute-start | bytes 1179656 | tf_op jit(solution)/shard_map/ppermute | solution.py:244
  25.7 15.3 %collective-permute-start.1 = (bf16[4,192,256]{2,1,0:T(8,128)(2,1)S(1)}, bf16[4,192,256]{2,1,0:T(8,128)(2,1)S(1)}, u32[]{:S(2)}, u32[]{:S(2)}) collective-permute-start(bf16[4,192,256]{2,1,0:T(8,128)(2,1)S(1)} %pad_maximum_fusion), channel_id=1, source_target_pairs={{0,4},{4,0},{1,5},{5,1},{2,6},{6,2},{3,7},{7,3},{8,12},{12,8},{9,1... | collective-permute-start | bytes 1179656 | tf_op jit(solution)/shard_map/ppermute | solution.py:244
  32.9 44.0 %all-to-all-start.1 = ((bf16[16,2,64,256]{3,2,1,0:T(8,128)(2,1)}), bf16[16,2,64,256]{3,2,1,0:T(8,128)(2,1)S(1)}, u32[]{:S(2)}, u32[]{:S(2)}) async-start(bf16[16,2,64,256]{3,2,1,0:T(8,128)(2,1)} %get-tuple-element.15), calls=%async_computation.1 | async-start | bytes 2097152 | tf_op jit(solution)/shard_map/all_to_all | solution.py:268
  41.1 9.8 %collective-permute-start.2 = (bf16[4,192,256]{2,1,0:T(8,128)(2,1)S(1)}, bf16[4,192,256]{2,1,0:T(8,128)(2,1)S(1)}, u32[]{:S(2)}, u32[]{:S(2)}) collective-permute-start(bf16[4,192,256]{2,1,0:T(8,128)(2,1)S(1)} %pad_maximum_fusion.2), channel_id=1, source_target_pairs={{0,32},{32,0},{1,33},{33,1},{2,34},{34,2},{3,35},{35,3},{4,36},{36... | collective-permute-start | bytes 1179656 | tf_op jit(solution)/shard_map/ppermute | solution.py:244
  44.3 22.3 %collective-permute-start.5 = (bf16[4,192,256]{2,1,0:T(8,128)(2,1)S(1)}, bf16[4,192,256]{2,1,0:T(8,128)(2,1)S(1)}, u32[]{:S(2)}, u32[]{:S(2)}) collective-permute-start(bf16[4,192,256]{2,1,0:T(8,128)(2,1)S(1)} %pad_maximum_fusion.1.refs_0_), channel_id=1, source_target_pairs={{0,2},{2,0},{1,3},{3,1},{4,6},{6,4},{5,7},{7,5},{8,10},{10,8},{9,1... | collective-permute-start | bytes 1179656 | tf_op jit(solution)/shard_map/ppermute | solution.py:244
  50.9 19.4 %collective-permute-start.6 = (bf16[4,192,256]{2,1,0:T(8,128)(2,1)S(1)}, bf16[4,192,256]{2,1,0:T(8,128)(2,1)S(1)}, u32[]{:S(2)}, u32[]{:S(2)}) collective-permute-start(bf16[4,192,256]{2,1,0:T(8,128)(2,1)S(1)} %collective-permute-done.2.refs_1_), channel_id=1, source_target_pairs={{0,2},{2,0},{1,3},{3,1},{4,6},{6,4},{5,7},{7,5},{8,10},{10,8},{9,1... | collective-permute-start | bytes 1179656 | tf_op jit(solution)/shard_map/ppermute | solution.py:244
  55.5 20.0 %collective-permute-start.3 = (bf16[4,192,256]{2,1,0:T(8,128)(2,1)S(1)}, bf16[4,192,256]{2,1,0:T(8,128)(2,1)S(1)}, u32[]{:S(2)}, u32[]{:S(2)}) collective-permute-start(bf16[4,192,256]{2,1,0:T(8,128)(2,1)S(1)} %pad_maximum_fusion.1.refs_0_), channel_id=1, source_target_pairs={{0,1},{1,0},{2,3},{3,2},{4,5},{5,4},{6,7},{7,6},{8,9},{9,8},{10,11... | collective-permute-start | bytes 1179656 | tf_op jit(solution)/shard_map/ppermute | solution.py:244
  64.6 10.9 %collective-permute-start.4 = (bf16[4,192,256]{2,1,0:T(8,128)(2,1)S(1)}, bf16[4,192,256]{2,1,0:T(8,128)(2,1)S(1)}, u32[]{:S(2)}, u32[]{:S(2)}) collective-permute-start(bf16[4,192,256]{2,1,0:T(8,128)(2,1)S(1)} %collective-permute-done.2.refs_1_), channel_id=1, source_target_pairs={{0,1},{1,0},{2,3},{3,2},{4,5},{5,4},{6,7},{7,6},{8,9},{9,8},{10,11... | collective-permute-start | bytes 1179656 | tf_op jit(solution)/shard_map/ppermute | solution.py:244
  66.5 8.9 %collective-permute-start.7 = (bf16[4,192,256]{2,1,0:T(8,128)(2,1)S(1)}, bf16[4,192,256]{2,1,0:T(8,128)(2,1)}, u32[]{:S(2)}, u32[]{:S(2)}) collective-permute-start(bf16[4,192,256]{2,1,0:T(8,128)(2,1)S(1)} %collective-permute-done.5.refs_4_), channel_id=1, source_target_pairs={{0,1},{1,0},{2,3},{3,2},{4,5},{5,4},{6,7},{7,6},{8,9},{9,8},{10,11... | collective-permute-start | bytes 1179656 | tf_op jit(solution)/shard_map/ppermute | solution.py:244
  70.3 6.6 %collective-permute-start.8 = (bf16[4,192,256]{2,1,0:T(8,128)(2,1)S(1)}, bf16[4,192,256]{2,1,0:T(8,128)(2,1)}, u32[]{:S(2)}, u32[]{:S(2)}) collective-permute-start(bf16[4,192,256]{2,1,0:T(8,128)(2,1)S(1)} %collective-permute-done.6.refs_5_), channel_id=1, source_target_pairs={{0,1},{1,0},{2,3},{3,2},{4,5},{5,4},{6,7},{7,6},{8,9},{9,8},{10,11... | collective-permute-start | bytes 1179656 | tf_op jit(solution)/shard_map/ppermute | solution.py:244
  81.5 3.7 %copy-start.6 = (bf16[48,24,2,256]{3,2,1,0:T(2,128)(2,1)S(1)}, bf16[48,24,2,256]{3,2,1,0:T(2,128)(2,1)}, u32[]{:S(2)}) copy-start(bf16[48,24,2,256]{3,2,1,0:T(2,128)(2,1)} %param.14) | copy-start | bytes 3538948
  81.5 23.8 %all-to-all-start.2 = ((f16[8,192,512]{2,1,0:T(8,128)(2,1)}), f16[8,192,512]{2,1,0:T(8,128)(2,1)S(1)}, u32[]{:S(2)}, u32[]{:S(2)}) async-start(f16[8,192,512]{2,1,0:T(8,128)(2,1)} %multiply_convert_fusion), calls=%async_computation.2 | async-start | bytes 3145728 | tf_op jit(solution)/shard_map/all_to_all | solution.py:272
  87.1 18.4 %copy-start.1 = (bf16[48,4,2048]{2,1,0:T(4,128)(2,1)S(1)}, bf16[48,4,2048]{2,1,0:T(4,128)(2,1)}, u32[]{:S(2)}) copy-start(bf16[48,4,2048]{2,1,0:T(4,128)(2,1)} %q_ref.1) | copy-start | bytes 2359300
  87.1 18.4 %copy-start.5 = (s32[48]{0:T(128)S(1)}, s32[48]{0:T(128)}, u32[]{:S(2)}) copy-start(s32[48]{0:T(128)} %lens_ref.1) | copy-start | bytes 580

commit v6 on v5

--- a/solution.py
+++ b/solution.py
@@ -205,11 +205,14 @@
         shifts = []
         for t, (rows, g, lens, q, k, v) in zip(turned, units):
             top = jnp.max(t + (base_t + length_bias(0, lens)), axis=0, keepdims=True)
-            shifts.append(jnp.where(eye, top, 0.0).astype(jnp.bfloat16))
+            high = top.astype(jnp.bfloat16).astype(jnp.float32)
+            shifts.append(
+                [jnp.where(eye, part, 0.0).astype(jnp.bfloat16) for part in (high, top - high)]
+            )
         scores = [
             lax.dot_general(
-                jnp.concatenate([q, shift], axis=1),
-                jnp.concatenate([k, minus], axis=1),
+                jnp.concatenate([q] + shift, axis=1),
+                jnp.concatenate([k, minus, minus], axis=1),
                 across,
                 preferred_element_type=jnp.float32,
             )

time: 109 us -> 110 us (level)
  no operation moved by 1% of the time
where the time goes in v6:
time: 110 us; the launch traced here: 109 us
  starting transfers between devices  61.1 us (56%)
  waiting for transfers between devices  33 us (30%)
  Pallas kernels  9.94 us (9%)
  other arithmetic  2 us (2%)
  local copies, waits for them, and re-layouts  1.95 us (2%)
    ppermute x9, starting transfers between devices, flipped(): return lax.ppermute(x, axis, [(0, 1), (1, 0)])  38.3 us
    all_to_all x1, waiting for transfers between devices, on_device(): partial = lax.all_to_all(partial, CUBE, 0, 0, tiled=True)  18.2 us
    ppermute x9, waiting for transfers between devices, flipped(): return lax.ppermute(x, axis, [(0, 1), (1, 0)])  12 us
    all_to_all x1, starting transfers between devices, on_device(): pieces = lax.all_to_all(pieces, FSDP, 0, 0, tiled=True)  11 us
    all_to_all x1, starting transfers between devices, on_device(): weight = lax.all_to_all(copies, FAR, 0, 0, tiled=True)  8.04 us
    all_to_all x1, starting transfers between devices, on_device(): partial = lax.all_to_all(partial, CUBE, 0, 0, tiled=True)  3.71 us
    pallas_call x1, Pallas kernels, attend(): pl.pallas_call(attend_kernel, out_shape=jax.ShapeDtypeStruct((ROWS, STEPS...  3.31 us
    pallas_call x1, Pallas kernels, project(): pl.pallas_call(project_kernel, out_shape=jax.ShapeDtypeStruct((8, TOK, 2...  2.98 us
  transfers between devices with their start and end apart: 12, of which 5 were waited for; matrix products, arithmetic and copies ran while one was open for 2% of the time, Pallas kernels for 2%

profile of v6, /device:TPU:1, one launch (start us, length us, event | category | flops | bytes accessed | tf_op | source)
XLA Modules:
  0.0 108.9 jit_solution(3806756305638426087)
XLA Ops:
  0.6 0.0 copy-start
  0.6 1.9 %by_owner.1 = bf16[8,2,64,256]{3,2,1,0:T(8,128)(2,1)} custom-call(bf16[1,2,8,64,256]{4,3,2,1,0:T(8,128)(2,1)} %bitcast.7), custom_call_target="tpu_custom_call" | custom-call | tf_op jit(solution)/shard_map/by_owner/pallas_call | solution.py:52
  2.6 0.0 copy-start.2
  2.6 0.0 copy-start.3
  2.6 0.0 copy-start.4
  2.6 11.0 %all-to-all-start = ((bf16[8,2,64,256]{3,2,1,0:T(8,128)(2,1)}), bf16[8,2,64,256]{3,2,1,0:T(8,128)(2,1)S(1)}, u32[]{:S(2)}, u32[]{:S(2)}) async-start(bf16[8,2,64,256]{3,2,1,0:T(8,128)(2,1)} %by_owner.1), calls=%async_computation | async-start | bytes 1048576 | tf_op jit(solution)/shard_map/all_to_all | solution.py:257
  13.6 0.0 copy-done
  13.6 0.4 split_features.1
  14.0 3.2 %collective-permute-start = (bf16[4,192,256]{2,1,0:T(8,128)(2,1)S(1)}, bf16[4,192,256]{2,1,0:T(8,128)(2,1)S(1)}, u32[]{:S(2)}, u32[]{:S(2)}) collective-permute-start(bf16[4,192,256]{2,1,0:T(8,128)(2,1)S(1)} %get-tuple-element.14), channel_id=1, source_target_pairs={{0,64},{64,0},{1,65},{65,1},{2,66},{66,2},{3,67},{67,3},{4,68},{68... | collective-permute-start | bytes 1179656 | tf_op jit(solution)/shard_map/ppermute | solution.py:247
  17.3 8.3 %collective-permute-done = bf16[4,192,256]{2,1,0:T(8,128)(2,1)S(1)} collective-permute-done((bf16[4,192,256]{2,1,0:T(8,128)(2,1)S(1)}, bf16[4,192,256]{2,1,0:T(8,128)(2,1)S(1)}, u32[]{:S(2)}, u32[]{:S(2)}) %collective-permute-start) | collective-permute-done | bytes 393248 | tf_op jit(solution)/shard_map/ppermute | solution.py:247
  25.7 3.1 %collective-permute-start.1 = (bf16[4,192,256]{2,1,0:T(8,128)(2,1)S(1)}, bf16[4,192,256]{2,1,0:T(8,128)(2,1)S(1)}, u32[]{:S(2)}, u32[]{:S(2)}) collective-permute-start(bf16[4,192,256]{2,1,0:T(8,128)(2,1)S(1)} %pad_maximum_fusion), channel_id=1, source_target_pairs={{0,4},{4,0},{1,5},{5,1},{2,6},{6,2},{3,7},{7,3},{8,12},{12,8},{9,1... | collective-permute-start | bytes 1179656 | tf_op jit(solution)/shard_map/ppermute | solution.py:247
  28.7 2.8 %all-to-all-done.g_ref = bf16[8,2,64,256]{3,2,1,0:T(8,128)(2,1)S(1)} async-done(((bf16[8,2,64,256]{3,2,1,0:T(8,128)(2,1)}), bf16[8,2,64,256]{3,2,1,0:T(8,128)(2,1)S(1)}, u32[]{:S(2)}, u32[]{:S(2)}) %all-to-all-start) | async-done | bytes 524320 | tf_op jit(solution)/shard_map/all_to_all | solution.py:257
  31.6 0.0 copy-done.2
  31.6 0.0 copy-done.3
  31.6 0.0 copy-done.4
  31.6 1.3 %adamw.1 = (f32[2,64,256]{2,1,0:T(8,128)}, f32[2,64,256]{2,1,0:T(8,128)}, f32[2,64,256]{2,1,0:T(8,128)}, bf16[16,2,64,256]{3,2,1,0:T(8,128)(2,1)}) custom-call(bf16[8,2,64,256]{3,2,1,0:T(8,128)(2,1)S(1)} %all-to-all-done.g_ref, f32[2,64,256]{2,1,0:T(8,128)S(1)} %copy-done.2, f32[2,64,256]{2,1,0:T(8,128)S(1)} %copy-done.3, f32[2,64,256]{2,1,0:T(8,128)S(1)} %copy-done.4), custom_call_target="tpu_custom_call" | custom-call | tf_op jit(solution)/shard_map/adamw/pallas_call | solution.py:82
  32.9 8.0 %all-to-all-start.1 = ((bf16[16,2,64,256]{3,2,1,0:T(8,128)(2,1)}), bf16[16,2,64,256]{3,2,1,0:T(8,128)(2,1)S(1)}, u32[]{:S(2)}, u32[]{:S(2)}) async-start(bf16[16,2,64,256]{3,2,1,0:T(8,128)(2,1)} %get-tuple-element.15), calls=%async_computation.1 | async-start | bytes 2097152 | tf_op jit(solution)/shard_map/all_to_all | solution.py:271
  41.0 0.0 collective-permute-done.1
  41.0 0.1 pad_maximum_fusion.2
  41.1 3.1 %collective-permute-start.2 = (bf16[4,192,256]{2,1,0:T(8,128)(2,1)S(1)}, bf16[4,192,256]{2,1,0:T(8,128)(2,1)S(1)}, u32[]{:S(2)}, u32[]{:S(2)}) collective-permute-start(bf16[4,192,256]{2,1,0:T(8,128)(2,1)S(1)} %pad_maximum_fusion.2), channel_id=1, source_target_pairs={{0,32},{32,0},{1,33},{33,1},{2,34},{34,2},{3,35},{35,3},{4,36},{36... | collective-permute-start | bytes 1179656 | tf_op jit(solution)/shard_map/ppermute | solution.py:247
  44.2 0.1 pad_maximum_fusion.1.refs_0_
  44.3 4.4 %collective-permute-start.5 = (bf16[4,192,256]{2,1,0:T(8,128)(2,1)S(1)}, bf16[4,192,256]{2,1,0:T(8,128)(2,1)S(1)}, u32[]{:S(2)}, u32[]{:S(2)}) collective-permute-start(bf16[4,192,256]{2,1,0:T(8,128)(2,1)S(1)} %pad_maximum_fusion.1.refs_0_), channel_id=1, source_target_pairs={{0,2},{2,0},{1,3},{3,1},{4,6},{6,4},{5,7},{7,5},{8,10},{10,8},{9,1... | collective-permute-start | bytes 1179656 | tf_op jit(solution)/shard_map/ppermute | solution.py:247
  48.6 2.2 %collective-permute-done.2.refs_1_ = bf16[4,192,256]{2,1,0:T(8,128)(2,1)S(1)} collective-permute-done((bf16[4,192,256]{2,1,0:T(8,128)(2,1)S(1)}, bf16[4,192,256]{2,1,0:T(8,128)(2,1)S(1)}, u32[]{:S(2)}, u32[]{:S(2)}) %collective-permute-start.2) | collective-permute-done | bytes 393248 | tf_op jit(solution)/shard_map/ppermute | solution.py:247
  50.9 4.6 %collective-permute-start.6 = (bf16[4,192,256]{2,1,0:T(8,128)(2,1)S(1)}, bf16[4,192,256]{2,1,0:T(8,128)(2,1)S(1)}, u32[]{:S(2)}, u32[]{:S(2)}) collective-permute-start(bf16[4,192,256]{2,1,0:T(8,128)(2,1)S(1)} %collective-permute-done.2.refs_1_), channel_id=1, source_target_pairs={{0,2},{2,0},{1,3},{3,1},{4,6},{6,4},{5,7},{7,5},{8,10},{10,8},{9,1... | collective-permute-start | bytes 1179656 | tf_op jit(solution)/shard_map/ppermute | solution.py:247
  55.5 9.1 %collective-permute-start.3 = (bf16[4,192,256]{2,1,0:T(8,128)(2,1)S(1)}, bf16[4,192,256]{2,1,0:T(8,128)(2,1)S(1)}, u32[]{:S(2)}, u32[]{:S(2)}) collective-permute-start(bf16[4,192,256]{2,1,0:T(8,128)(2,1)S(1)} %pad_maximum_fusion.1.refs_0_), channel_id=1, source_target_pairs={{0,1},{1,0},{2,3},{3,2},{4,5},{5,4},{6,7},{7,6},{8,9},{9,8},{10,11... | collective-permute-start | bytes 1179656 | tf_op jit(solution)/shard_map/ppermute | solution.py:247
  64.6 1.9 %collective-permute-start.4 = (bf16[4,192,256]{2,1,0:T(8,128)(2,1)S(1)}, bf16[4,192,256]{2,1,0:T(8,128)(2,1)S(1)}, u32[]{:S(2)}, u32[]{:S(2)}) collective-permute-start(bf16[4,192,256]{2,1,0:T(8,128)(2,1)S(1)} %collective-permute-done.2.refs_1_), channel_id=1, source_target_pairs={{0,1},{1,0},{2,3},{3,2},{4,5},{5,4},{6,7},{7,6},{8,9},{9,8},{10,11... | collective-permute-start | bytes 1179656 | tf_op jit(solution)/shard_map/ppermute | solution.py:247
  66.5 0.0 collective-permute-done.5.refs_4_
  66.5 3.7 %collective-permute-start.7 = (bf16[4,192,256]{2,1,0:T(8,128)(2,1)S(1)}, bf16[4,192,256]{2,1,0:T(8,128)(2,1)}, u32[]{:S(2)}, u32[]{:S(2)}) collective-permute-start(bf16[4,192,256]{2,1,0:T(8,128)(2,1)S(1)} %collective-permute-done.5.refs_4_), channel_id=1, source_target_pairs={{0,1},{1,0},{2,3},{3,2},{4,5},{5,4},{6,7},{7,6},{8,9},{9,8},{10,11... | collective-permute-start | bytes 1179656 | tf_op jit(solution)/shard_map/ppermute | solution.py:247
  70.3 0.0 collective-permute-done.6.refs_5_
  70.3 5.2 %collective-permute-start.8 = (bf16[4,192,256]{2,1,0:T(8,128)(2,1)S(1)}, bf16[4,192,256]{2,1,0:T(8,128)(2,1)}, u32[]{:S(2)}, u32[]{:S(2)}) collective-permute-start(bf16[4,192,256]{2,1,0:T(8,128)(2,1)S(1)} %collective-permute-done.6.refs_5_), channel_id=1, source_target_pairs={{0,1},{1,0},{2,3},{3,2},{4,5},{5,4},{6,7},{7,6},{8,9},{9,8},{10,11... | collective-permute-start | bytes 1179656 | tf_op jit(solution)/shard_map/ppermute | solution.py:247
  75.5 0.0 collective-permute-done.3.refs_2_
  75.5 0.0 collective-permute-done.7.refs_6_
  75.5 0.0 collective-permute-done.4.refs_3_
  75.5 1.4 %collective-permute-done.8.refs_7_ = bf16[4,192,256]{2,1,0:T(8,128)(2,1)} collective-permute-done((bf16[4,192,256]{2,1,0:T(8,128)(2,1)S(1)}, bf16[4,192,256]{2,1,0:T(8,128)(2,1)}, u32[]{:S(2)}, u32[]{:S(2)}) %collective-permute-start.8) | collective-permute-done | bytes 393248 | tf_op jit(solution)/shard_map/ppermute | solution.py:247
  76.9 0.0 all-to-all-done.1.refs_8_
  76.9 3.0 %project.1 = f32[8,192,512]{2,1,0:T(8,128)S(1)} custom-call(s32[1]{0:T(128)} %bitcast.1.me_ref, s32[1]{0:T(128)} %bitcast.2.t_ref, bf16[4,192,256]{2,1,0:T(8,128)(2,1)S(1)} %pad_maximum_fusion.1.refs_0_, bf16[4,192,256]{2,1,0:T(8,128)(2,1)S(1)} %collective-permute-done.2.refs_1_, bf16[4,192,256]{2,1,0:T(8,128)(2,1)S(1)} %collective-permute-done.3.refs_2_, ...), custom_call_target="tpu_custom_call" | custom-call | tf_op jit(solution)/shard_map/project/pallas_call | solution.py:144
  79.9 1.6 %multiply_convert_fusion = f16[8,192,512]{2,1,0:T(8,128)(2,1)} fusion(f32[8,192,512]{2,1,0:T(8,128)S(1)} %project.1), kind=kLoop, calls=%fused_computation.1 | loop fusion | flops 1572864 | bytes 4718592 | tf_op jit(solution)/shard_map/convert_element_type | solution.py:274
  81.5 0.0 copy-start.6
  81.5 3.7 %all-to-all-start.2 = ((f16[8,192,512]{2,1,0:T(8,128)(2,1)}), f16[8,192,512]{2,1,0:T(8,128)(2,1)S(1)}, u32[]{:S(2)}, u32[]{:S(2)}) async-start(f16[8,192,512]{2,1,0:T(8,128)(2,1)} %multiply_convert_fusion), calls=%async_computation.2 | async-start | bytes 3145728 | tf_op jit(solution)/shard_map/all_to_all | solution.py:275
  85.2 0.0 copy-done.6
  85.3 1.6 %fusion = (bf16[48,24,1,256]{3,2,1,0:T(2,128)(2,1)S(1)}, bf16[48,24,1,256]{3,2,1,0:T(2,128)(2,1)S(1)}) fusion(bf16[48,24,2,256]{3,2,1,0:T(2,128)(2,1)S(1)} %copy-done.6), kind=kLoop, calls=%fused_computation.6 | loop fusion | bytes 2359296 | tf_op jit(solution)/shard_map/slice | solution.py:279
  86.9 0.1 copy.15
  87.0 0.1 copy.14
  87.1 0.0 copy-start.1
  87.1 0.0 copy-start.5
  87.1 18.2 %all-to-all-done.2 = f16[8,192,512]{2,1,0:T(8,128)(2,1)S(1)} async-done(((f16[8,192,512]{2,1,0:T(8,128)(2,1)}), f16[8,192,512]{2,1,0:T(8,128)(2,1)S(1)}, u32[]{:S(2)}, u32[]{:S(2)}) %all-to-all-start.2) | async-done | bytes 1572896 | tf_op jit(solution)/shard_map/all_to_all | solution.py:275
  105.3 0.2 convert_reduce_fusion
  105.5 0.0 copy-done.1
  105.5 0.0 copy-done.5
  105.6 3.3 %attend.1 = bf16[48,4,2048]{2,1,0:T(4,128)(2,1)} custom-call(s32[48]{0:T(128)S(1)} %copy-done.5, bf16[192,512]{1,0:T(8,128)(2,1)S(1)} %multiply_convert_fusion.1.fresh_ref, bf16[48,4,2048]{2,1,0:T(4,128)(2,1)S(1)} %copy-done.1, bf16[1152,256]{1,0:T(8,128)(2,1)S(1)} %bitcast.6, bf16[1152,256]{1,0:T(8,128)(2,1)S(1)} %bitcast.5), custom_call_target="tpu_custom_call" | custom-call | tf_op jit(solution)/shard_map/attend/pallas_call | solution.py:236
  (7 shorter events, 0.2 us)
Async XLA Ops:
  0.6 13.0 %copy-start = (bf16[48,4,2048]{2,1,0:T(4,128)(2,1)S(1)}, bf16[48,4,2048]{2,1,0:T(4,128)(2,1)}, u32[]{:S(2)}) copy-start(bf16[48,4,2048]{2,1,0:T(4,128)(2,1)} %x_ref.1) | copy-start | bytes 2359300
  2.6 29.0 %copy-start.2 = (f32[2,64,256]{2,1,0:T(8,128)S(1)}, f32[2,64,256]{2,1,0:T(8,128)}, u32[]{:S(2)}) copy-start(f32[2,64,256]{2,1,0:T(8,128)} %w_ref.1) | copy-start | bytes 393220
  2.6 29.0 %copy-start.3 = (f32[2,64,256]{2,1,0:T(8,128)S(1)}, f32[2,64,256]{2,1,0:T(8,128)}, u32[]{:S(2)}) copy-start(f32[2,64,256]{2,1,0:T(8,128)} %one_ref.1) | copy-start | bytes 393220
  2.6 29.0 %copy-start.4 = (f32[2,64,256]{2,1,0:T(8,128)S(1)}, f32[2,64,256]{2,1,0:T(8,128)}, u32[]{:S(2)}) copy-start(f32[2,64,256]{2,1,0:T(8,128)} %two_ref.1) | copy-start | bytes 393220
  2.6 29.0 %all-to-all-start = ((bf16[8,2,64,256]{3,2,1,0:T(8,128)(2,1)}), bf16[8,2,64,256]{3,2,1,0:T(8,128)(2,1)S(1)}, u32[]{:S(2)}, u32[]{:S(2)}) async-start(bf16[8,2,64,256]{3,2,1,0:T(8,128)(2,1)} %by_owner.1), calls=%async_computation | async-start | bytes 1048576 | tf_op jit(solution)/shard_map/all_to_all | solution.py:257
  14.0 11.6 %collective-permute-start = (bf16[4,192,256]{2,1,0:T(8,128)(2,1)S(1)}, bf16[4,192,256]{2,1,0:T(8,128)(2,1)S(1)}, u32[]{:S(2)}, u32[]{:S(2)}) collective-permute-start(bf16[4,192,256]{2,1,0:T(8,128)(2,1)S(1)} %get-tuple-element.14), channel_id=1, source_target_pairs={{0,64},{64,0},{1,65},{65,1},{2,66},{66,2},{3,67},{67,3},{4,68},{68... | collective-permute-start | bytes 1179656 | tf_op jit(solution)/shard_map/ppermute | solution.py:247
  25.7 15.3 %collective-permute-start.1 = (bf16[4,192,256]{2,1,0:T(8,128)(2,1)S(1)}, bf16[4,192,256]{2,1,0:T(8,128)(2,1)S(1)}, u32[]{:S(2)}, u32[]{:S(2)}) collective-permute-start(bf16[4,192,256]{2,1,0:T(8,128)(2,1)S(1)} %pad_maximum_fusion), channel_id=1, source_target_pairs={{0,4},{4,0},{1,5},{5,1},{2,6},{6,2},{3,7},{7,3},{8,12},{12,8},{9,1... | collective-permute-start | bytes 1179656 | tf_op jit(solution)/shard_map/ppermute | solution.py:247
  32.9 44.0 %all-to-all-start.1 = ((bf16[16,2,64,256]{3,2,1,0:T(8,128)(2,1)}), bf16[16,2,64,256]{3,2,1,0:T(8,128)(2,1)S(1)}, u32[]{:S(2)}, u32[]{:S(2)}) async-start(bf16[16,2,64,256]{3,2,1,0:T(8,128)(2,1)} %get-tuple-element.15), calls=%async_computation.1 | async-start | bytes 2097152 | tf_op jit(solution)/shard_map/all_to_all | solution.py:271
  41.1 9.8 %collective-permute-start.2 = (bf16[4,192,256]{2,1,0:T(8,128)(2,1)S(1)}, bf16[4,192,256]{2,1,0:T(8,128)(2,1)S(1)}, u32[]{:S(2)}, u32[]{:S(2)}) collective-permute-start(bf16[4,192,256]{2,1,0:T(8,128)(2,1)S(1)} %pad_maximum_fusion.2), channel_id=1, source_target_pairs={{0,32},{32,0},{1,33},{33,1},{2,34},{34,2},{3,35},{35,3},{4,36},{36... | collective-permute-start | bytes 1179656 | tf_op jit(solution)/shard_map/ppermute | solution.py:247
  44.3 22.3 %collective-permute-start.5 = (bf16[4,192,256]{2,1,0:T(8,128)(2,1)S(1)}, bf16[4,192,256]{2,1,0:T(8,128)(2,1)S(1)}, u32[]{:S(2)}, u32[]{:S(2)}) collective-permute-start(bf16[4,192,256]{2,1,0:T(8,128)(2,1)S(1)} %pad_maximum_fusion.1.refs_0_), channel_id=1, source_target_pairs={{0,2},{2,0},{1,3},{3,1},{4,6},{6,4},{5,7},{7,5},{8,10},{10,8},{9,1... | collective-permute-start | bytes 1179656 | tf_op jit(solution)/shard_map/ppermute | solution.py:247
  50.9 19.4 %collective-permute-start.6 = (bf16[4,192,256]{2,1,0:T(8,128)(2,1)S(1)}, bf16[4,192,256]{2,1,0:T(8,128)(2,1)S(1)}, u32[]{:S(2)}, u32[]{:S(2)}) collective-permute-start(bf16[4,192,256]{2,1,0:T(8,128)(2,1)S(1)} %collective-permute-done.2.refs_1_), channel_id=1, source_target_pairs={{0,2},{2,0},{1,3},{3,1},{4,6},{6,4},{5,7},{7,5},{8,10},{10,8},{9,1... | collective-permute-start | bytes 1179656 | tf_op jit(solution)/shard_map/ppermute | solution.py:247
  55.5 20.0 %collective-permute-start.3 = (bf16[4,192,256]{2,1,0:T(8,128)(2,1)S(1)}, bf16[4,192,256]{2,1,0:T(8,128)(2,1)S(1)}, u32[]{:S(2)}, u32[]{:S(2)}) collective-permute-start(bf16[4,192,256]{2,1,0:T(8,128)(2,1)S(1)} %pad_maximum_fusion.1.refs_0_), channel_id=1, source_target_pairs={{0,1},{1,0},{2,3},{3,2},{4,5},{5,4},{6,7},{7,6},{8,9},{9,8},{10,11... | collective-permute-start | bytes 1179656 | tf_op jit(solution)/shard_map/ppermute | solution.py:247
  64.6 10.9 %collective-permute-start.4 = (bf16[4,192,256]{2,1,0:T(8,128)(2,1)S(1)}, bf16[4,192,256]{2,1,0:T(8,128)(2,1)S(1)}, u32[]{:S(2)}, u32[]{:S(2)}) collective-permute-start(bf16[4,192,256]{2,1,0:T(8,128)(2,1)S(1)} %collective-permute-done.2.refs_1_), channel_id=1, source_target_pairs={{0,1},{1,0},{2,3},{3,2},{4,5},{5,4},{6,7},{7,6},{8,9},{9,8},{10,11... | collective-permute-start | bytes 1179656 | tf_op jit(solution)/shard_map/ppermute | solution.py:247
  66.5 8.9 %collective-permute-start.7 = (bf16[4,192,256]{2,1,0:T(8,128)(2,1)S(1)}, bf16[4,192,256]{2,1,0:T(8,128)(2,1)}, u32[]{:S(2)}, u32[]{:S(2)}) collective-permute-start(bf16[4,192,256]{2,1,0:T(8,128)(2,1)S(1)} %collective-permute-done.5.refs_4_), channel_id=1, source_target_pairs={{0,1},{1,0},{2,3},{3,2},{4,5},{5,4},{6,7},{7,6},{8,9},{9,8},{10,11... | collective-permute-start | bytes 1179656 | tf_op jit(solution)/shard_map/ppermute | solution.py:247
  70.3 6.6 %collective-permute-start.8 = (bf16[4,192,256]{2,1,0:T(8,128)(2,1)S(1)}, bf16[4,192,256]{2,1,0:T(8,128)(2,1)}, u32[]{:S(2)}, u32[]{:S(2)}) collective-permute-start(bf16[4,192,256]{2,1,0:T(8,128)(2,1)S(1)} %collective-permute-done.6.refs_5_), channel_id=1, source_target_pairs={{0,1},{1,0},{2,3},{3,2},{4,5},{5,4},{6,7},{7,6},{8,9},{9,8},{10,11... | collective-permute-start | bytes 1179656 | tf_op jit(solution)/shard_map/ppermute | solution.py:247
  81.5 3.7 %copy-start.6 = (bf16[48,24,2,256]{3,2,1,0:T(2,128)(2,1)S(1)}, bf16[48,24,2,256]{3,2,1,0:T(2,128)(2,1)}, u32[]{:S(2)}) copy-start(bf16[48,24,2,256]{3,2,1,0:T(2,128)(2,1)} %param.14) | copy-start | bytes 3538948
  81.5 23.8 %all-to-all-start.2 = ((f16[8,192,512]{2,1,0:T(8,128)(2,1)}), f16[8,192,512]{2,1,0:T(8,128)(2,1)S(1)}, u32[]{:S(2)}, u32[]{:S(2)}) async-start(f16[8,192,512]{2,1,0:T(8,128)(2,1)} %multiply_convert_fusion), calls=%async_computation.2 | async-start | bytes 3145728 | tf_op jit(solution)/shard_map/all_to_all | solution.py:275
  87.1 18.4 %copy-start.1 = (bf16[48,4,2048]{2,1,0:T(4,128)(2,1)S(1)}, bf16[48,4,2048]{2,1,0:T(4,128)(2,1)}, u32[]{:S(2)}) copy-start(bf16[48,4,2048]{2,1,0:T(4,128)(2,1)} %q_ref.1) | copy-start | bytes 2359300
  87.1 18.4 %copy-start.5 = (s32[48]{0:T(128)S(1)}, s32[48]{0:T(128)}, u32[]{:S(2)}) copy-start(s32[48]{0:T(128)} %lens_ref.1) | copy-start | bytes 580
